TPU v7x, 512 devices: a whole 4x4x16 slice. The times are simulated.
512 devices in a mesh: dp: 8 (over y, x_hi), expert: 64 (over x_lo, z, core).
Axes of the slice: x: 4 (x_hi: 2, x_lo: 2; x = x_hi * 2 + x_lo), y: 4, z: 16, core: 2. Of those that a mesh axis runs over, the one named last changes fastest.
Arguments:
- tokens: bfloat16 [8192, 3584], P('expert'), may hold values from -6 to 6
- routes: int32 [8192, 2], P('expert'), may hold values from 0 to 31, all different within a row; in each aligned block of 128 rows (0 to 127, 128 to 255, ...) at most 10 rows name the same one
- gate_weights: float32 [8192, 2], P('expert'), may hold values from 0.2 to 1
- w_dense_gate: bfloat16 [3584, 2432], P('expert', 'dp'), may hold values from -0.09375 to 0.09375
- w_dense_up: bfloat16 [3584, 2432], P('expert', 'dp'), may hold values from -0.09375 to 0.09375
- w_dense_down: bfloat16 [2432, 3584], P('dp', 'expert'), may hold values from -0.125 to 0.125
- w_exp_gate: bfloat16 [8, 64, 3584, 152], P('dp', 'expert'), may hold values from -0.09375 to 0.09375
- w_exp_up: bfloat16 [8, 64, 3584, 152], P('dp', 'expert'), may hold values from -0.09375 to 0.09375
- w_exp_down: bfloat16 [8, 64, 152, 3584], P('dp', 'expert'), may hold values from -0.125 to 0.125
Outputs:
- mixed: bfloat16 [8192, 3584], P('expert', 'dp')
Inputs may be any that keep to these rules, and one draw needn't show every extreme that they name: `routes`: the two experts of a token differ. Among the rows of one device, no expert is named more than 10 times, and in every draw some expert is named exactly 10 times by some device's rows.
All inputs are finite; a program needn't handle non-finite values.
Results may differ from a plain program's by a relative error of at most 0.019.
Values may be sent and summed in bfloat16 or wider, within the bound.
A program may use at most 128 MiB of HBM per device.

v0:
```python
import jax
import jax.numpy as jnp
from jax import lax
from jax.sharding import PartitionSpec as P

TOP = 2


def per_device(
    tokens,
    routes,
    gate_weights,
    w_dense_gate,
    w_dense_up,
    w_dense_down,
    w_exp_gate,
    w_exp_up,
    w_exp_down,
):
    tok_rows = tokens.shape[0]
    width = tokens.shape[1]
    devices = lax.axis_size("expert")
    groups = devices // 2
    capacity = 2 * max(1, tok_rows * TOP * 5 // (8 * groups))
    places = groups * capacity
    flat_route = routes.reshape(-1)
    owners = (flat_route[:, None] == jnp.arange(groups, dtype=jnp.int32)[None, :]).astype(jnp.int32)
    earlier = jnp.cumsum(owners, axis=0) - owners
    ranking = jnp.sum(earlier * owners, axis=1)
    target = flat_route * capacity + ranking
    selector = (target[:, None] == jnp.arange(places, dtype=jnp.int32)[None, :]).astype(
        jnp.bfloat16
    )
    token_select = jnp.sum(selector.reshape(tok_rows, TOP, places), axis=1)
    outgoing = jnp.einsum("tp,td->pd", token_select, tokens, preferred_element_type=jnp.float32)
    outgoing = outgoing.astype(jnp.bfloat16).reshape(groups, capacity, width)
    local_gate = w_exp_gate[0, 0]
    local_up = w_exp_up[0, 0]
    local_down = w_exp_down[0, 0]
    doubled = jnp.repeat(outgoing, 2, axis=0)
    arrived = lax.all_to_all(doubled, "expert", split_axis=0, concat_axis=0, tiled=True)
    flat_rows = arrived.reshape(-1, width)
    gate = jnp.dot(flat_rows, local_gate, preferred_element_type=jnp.float32)
    up = jnp.dot(flat_rows, local_up, preferred_element_type=jnp.float32)
    hidden = (jax.nn.silu(gate) * up).astype(jnp.bfloat16)
    result = jnp.dot(hidden, local_down, preferred_element_type=jnp.float32)
    result = result.reshape(arrived.shape[:-1] + (width,))
    returned = lax.all_to_all(
        result.astype(jnp.bfloat16), "expert", split_axis=0, concat_axis=0, tiled=True
    ).astype(result.dtype)
    merged = jnp.sum(returned.reshape(groups, 2, capacity, width), axis=1).astype(jnp.bfloat16)
    slot_ids = jnp.arange(places, dtype=jnp.int32)
    slot_group = slot_ids // capacity
    slot_rank = slot_ids % capacity
    matches = (flat_route[:, None] == slot_group[None, :]) & (
        ranking[:, None] == slot_rank[None, :]
    )
    pair_select = matches.astype(jnp.bfloat16)
    picked = jnp.dot(pair_select, merged.reshape(-1, width), preferred_element_type=jnp.float32)
    weighted = jnp.sum(picked.reshape(tok_rows, TOP, width) * gate_weights[:, :, None], axis=1)
    dense_gate = jnp.dot(
        tokens,
        lax.all_gather(w_dense_gate, "expert", axis=0, tiled=True),
        preferred_element_type=jnp.float32,
    )
    dense_up = jnp.dot(
        tokens,
        lax.all_gather(w_dense_up, "expert", axis=0, tiled=True),
        preferred_element_type=jnp.float32,
    )
    dense_hidden = (jax.nn.silu(dense_gate) * dense_up).astype(jnp.bfloat16)
    dense_part = jnp.dot(
        dense_hidden,
        lax.all_gather(w_dense_down, "expert", axis=1, tiled=True),
        preferred_element_type=jnp.float32,
    )
    slice_term = dense_part + weighted
    return lax.psum_scatter(slice_term.astype(jnp.bfloat16), "dp", scatter_dimension=1, tiled=True)


def solution(mesh):
    in_specs = (
        P("expert", None),
        P("expert", None),
        P("expert", None),
        P("expert", "dp"),
        P("expert", "dp"),
        P("dp", "expert"),
        P("dp", "expert", None, None),
        P("dp", "expert", None, None),
        P("dp", "expert", None, None),
    )
    out_specs = P("expert", "dp")
    return jax.shard_map(
        per_device, mesh=mesh, in_specs=in_specs, out_specs=out_specs, check_vma=False
    )
```

profile of v0, /device:TPU:32, one launch (start us, length us, event | category | flops | bytes accessed | tf_op | source)
XLA Modules:
  0.0 985.9 jit_solution(3601620394329934930)
XLA Ops:
  6.5 0.9 copy.45
  7.6 0.1 eq.82
  7.7 0.6 reduce-window.6
  8.3 0.2 slice_reduce_fusion
  8.6 0.1 eq.90
  8.8 0.7 multiply_add_fusion
  9.6 1.9 convolution_convert_fusion.1
  11.5 2.6 reshape.105
  14.1 2.9 broadcast_in_dim.2
  17.1 336.8 %all_to_all.10 = bf16[64,10,3584]{2,1,0:T(8,128)(2,1)} all-to-all(bf16[64,10,3584]{2,1,0:T(8,128)(2,1)S(1)} %bitcast.43), channel_id=1, replica_groups=mesh['dp'=8,'expert'=64] {'expert'}, dimensions={0} | all-to-all | bytes 9175040 | tf_op jit(solution)/shard_map/all_to_all | solution.py:41
  353.9 8.1 reshape.107
  362.0 4.0 fusion.6
  366.0 1.6 fusion.2
  367.6 0.2 copy.50
  368.0 1.4 convolution_convert_fusion
  369.3 5.8 copy.52
  375.1 9.7 all-to-all-start.1
  384.9 0.7 all-gather.4.cloned.1.call-update
  385.6 0.7 all-gather.6.cloned.1.call-update
  386.4 0.7 all-gather.8.cloned.1.call-update
  387.1 0.2 reduce-scatter.2.cloned.1.call-start
  387.3 214.4 %all-gather.4.cloned.1.call-done = bf16[3584,304]{1,0:T(8,128)(2,1)} async-done(((bf16[56,304]{1,0:T(8,128)(2,1)}), bf16[3584,304]{1,0:T(8,128)(2,1)}) %all-gather.4.cloned.1.call-update) | async-done | bytes 2179088 | tf_op jit(solution)/shard_map/all_gather | solution.py:63
  601.7 2.9 fusion.36
  604.6 120.1 %all-to-all-done.1 = bf16[64,10,3584]{2,1,0:T(8,128)(2,1)} async-done(((bf16[64,10,3584]{2,1,0:T(8,128)(2,1)}), bf16[64,10,3584]{2,1,0:T(8,128)(2,1)}, u32[]{:S(2)}, u32[]{:S(2)}) %all-to-all-start.1) | async-done | bytes 4587552 | tf_op jit(solution)/shard_map/all_to_all | solution.py:48
  724.7 8.1 bitcast_reduce_fusion
  732.8 4.5 reshape.111
  737.4 4.3 fusion.1
  741.6 2.8 copy.55
  744.4 21.4 %all-gather.6.cloned.1.call-done = bf16[3584,304]{1,0:T(8,128)(2,1)} async-done(((bf16[56,304]{1,0:T(8,128)(2,1)}), bf16[3584,304]{1,0:T(8,128)(2,1)}) %all-gather.6.cloned.1.call-update) | async-done | bytes 2179088 | tf_op jit(solution)/shard_map/all_gather | solution.py:68
  765.8 123.1 %all-gather.8.cloned.1.call-done = bf16[304,3584]{0,1:T(8,128)(2,1)} async-done(((bf16[304,56]{0,1:T(8,128)(2,1)}), bf16[304,3584]{0,1:T(8,128)(2,1)}) %all-gather.8.cloned.1.call-update) | async-done | bytes 2179088 | tf_op jit(solution)/shard_map/all_gather | solution.py:74
  889.0 6.9 fusion
  895.9 83.5 %reduce-scatter.2.cloned.1.call-done = bf16[128,448]{0,1:T(8,128)(2,1)} async-done(((bf16[128,3584]{0,1:T(8,128)(2,1)}), bf16[128,448]{0,1:T(8,128)(2,1)}) %reduce-scatter.2.cloned.1.call-update) | async-done | bytes 114704 | tf_op jit(solution)/shard_map/reduce_scatter | solution.py:78
  (29 shorter events, 0.7 us)
Async XLA Ops:
  6.5 361.4 %copy-start = (bf16[1,1,152,3584]{3,2,1,0:T(8,128)(2,1)S(1)}, bf16[1,1,152,3584]{3,2,1,0:T(8,128)(2,1)}, u32[]{:S(2)}) copy-start(bf16[1,1,152,3584]{3,2,1,0:T(8,128)(2,1)} %param.17) | copy-start | bytes 3268612
  353.9 8.1 copy-start.5
  362.0 4.0 copy-start.3
  362.0 4.0 copy-start.6
  375.1 226.6 %copy-start.2 = (bf16[128,3584]{1,0:T(8,128)(2,1)S(1)}, bf16[128,3584]{1,0:T(8,128)(2,1)}, u32[]{:S(2)}) copy-start(bf16[128,3584]{1,0:T(8,128)(2,1)} %param.9) | copy-start | bytes 2752516
  375.1 349.6 %all-to-all-start.1 = ((bf16[64,10,3584]{2,1,0:T(8,128)(2,1)}), bf16[64,10,3584]{2,1,0:T(8,128)(2,1)}, u32[]{:S(2)}, u32[]{:S(2)}) async-start(bf16[64,10,3584]{2,1,0:T(8,128)(2,1)} %copy.52), calls=%async_computation.1 | async-start | bytes 14680064 | tf_op jit(solution)/shard_map/all_to_all | solution.py:48
  384.9 216.9 %all-gather.4.cloned.1.call-start = ((), (), s32[]{:S(2)}) async-start(), calls=%async_computation.3 | async-start | bytes 2795520 | tf_op jit(solution)/shard_map/all_gather | solution.py:63
  385.6 380.2 %all-gather.6.cloned.1.call-start = ((), (), s32[]{:S(2)}) async-start(), calls=%async_computation.4 | async-start | bytes 2795520 | tf_op jit(solution)/shard_map/all_gather | solution.py:68
  386.3 502.6 %all-gather.8.cloned.1.call-start = ((), (), s32[]{:S(2)}) async-start(), calls=%async_computation.5 | async-start | bytes 2795520 | tf_op jit(solution)/shard_map/all_gather | solution.py:74
  387.1 592.3 %reduce-scatter.2.cloned.1.call-start = ((), (), s32[]{:S(2)}) async-start(), calls=%async_computation.6 | async-start | bytes 1032192 | tf_op jit(solution)/shard_map/reduce_scatter | solution.py:78
  732.8 4.5 copy-start.4
  732.8 4.5 copy-start.7
  889.0 90.4 %copy-start.1 = (bf16[1,1,152,3584]{3,2,1,0:T(8,128)(2,1)S(1)}, bf16[1,1,152,3584]{3,2,1,0:T(8,128)(2,1)}, u32[]{:S(2)}) copy-start(bf16[1,1,152,3584]{3,2,1,0:T(8,128)(2,1)} %param.17) | copy-start | bytes 3268612
Sparse Core Ops, SparseCore 0:
  387.8 213.8 all-gather.3
  603.9 161.9 all-gather.5
  768.0 120.9 all-gather.7
  896.0 83.3 reduce-scatter.1
where the time goes:
time: 987 us; the launch traced here: 986 us
  waiting for transfers between devices  565 us (57%)
  blocking collectives  337 us (34%)
  local copies, waits for them, and re-layouts  28.6 us (3%)
  matrix products  22.9 us (2%)
  between operations  13.3 us (1%)
  starting transfers between devices  10.1 us (1%)
    all_to_all x1, blocking collectives, per_device(): lax.all_to_all(doubled, 'expert', split_axis=0, concat_axis=0, tiled=True)  337 us
    all_gather x1, waiting for transfers between devices, per_device(): lax.all_gather(w_dense_gate, 'expert', axis=0, tiled=True)  214 us
    all_gather x1, waiting for transfers between devices, per_device(): lax.all_gather(w_dense_down, 'expert', axis=1, tiled=True)  123 us
    all_to_all x1, waiting for transfers between devices, per_device(): lax.all_to_all(result.astype(jnp.bfloat16), 'expert', split_axis=0, conca...  120 us
    reduce_scatter x1, waiting for transfers between devices, per_device(): lax.psum_scatter(slice_term.astype(jnp.bfloat16), 'dp', scatter_dimension...  83.5 us
    all_gather x1, waiting for transfers between devices, per_device(): lax.all_gather(w_dense_up, 'expert', axis=0, tiled=True)  21.4 us
  transfers between devices with their start and end apart: 5, of which 5 were waited for; matrix products, arithmetic and copies ran while one was open for 2% of the time, Pallas kernels for 0%

commit v1 on v0

v1 whole, which is shorter than its diff:
```python
import jax
import jax.numpy as jnp
from jax import lax
from jax.sharding import Mesh, PartitionSpec as P

TOP = 2
CAP = 10


def per_device(
    tokens,
    routes,
    gate_weights,
    w_dense_gate,
    w_dense_up,
    w_dense_down,
    w_exp_gate,
    w_exp_up,
    w_exp_down,
):
    tok_rows, width = tokens.shape
    n_dp = lax.axis_size("dp")
    groups = lax.axis_size("group")
    devices = 2 * groups
    part = width // n_dp
    half = part // 2
    places = groups * CAP
    me_dp = lax.axis_index("dp")

    flat_route = routes.reshape(-1)
    owners = (flat_route[:, None] == jnp.arange(groups, dtype=jnp.int32)[None, :]).astype(jnp.int32)
    earlier = jnp.cumsum(owners, axis=0) - owners
    ranking = jnp.sum(earlier * owners, axis=1)
    target = flat_route * CAP + ranking
    selector = target[:, None] == jnp.arange(places, dtype=jnp.int32)[None, :]
    selector = selector.reshape(tok_rows, TOP, places)
    token_select = jnp.sum(selector.astype(jnp.bfloat16), axis=1)

    mine = lax.dynamic_slice_in_dim(tokens, me_dp * part, part, axis=1)
    outgoing = jnp.einsum("tp,td->pd", token_select, mine, preferred_element_type=jnp.float32)
    outgoing = outgoing.astype(jnp.bfloat16).reshape(groups, CAP, 2, half)
    outgoing = outgoing.transpose(0, 2, 1, 3).reshape(devices, CAP, half)
    arrived = lax.all_to_all(outgoing, ("group", "core"), split_axis=0, concat_axis=0, tiled=True)
    rows = arrived.reshape(devices * CAP, half)
    allcols = lax.all_gather(rows, ("dp", "core"), axis=0, tiled=False)
    allcols = allcols.reshape(n_dp * 2, devices * CAP, half)
    x = allcols.transpose(1, 0, 2).reshape(devices * CAP, width)
    gate = jnp.dot(x, w_exp_gate[0, 0], preferred_element_type=jnp.float32)
    up = jnp.dot(x, w_exp_up[0, 0], preferred_element_type=jnp.float32)
    hidden = (jax.nn.silu(gate) * up).astype(jnp.bfloat16)
    result = jnp.dot(hidden, w_exp_down[0, 0], preferred_element_type=jnp.float32)
    result = result.astype(jnp.bfloat16)
    summed = lax.psum_scatter(result, ("dp", "core"), scatter_dimension=1, tiled=True)
    summed = summed.reshape(devices, CAP, half)
    returned = lax.all_to_all(summed, ("group", "core"), split_axis=0, concat_axis=0, tiled=True)
    returned = returned.reshape(groups, 2, CAP, half).transpose(0, 2, 1, 3).reshape(places, part)
    mix = jnp.sum(selector.astype(jnp.float32) * gate_weights[:, :, None], axis=1)
    weighted = jnp.dot(mix, returned.astype(jnp.float32), preferred_element_type=jnp.float32)

    tok_axes = ("group", "core")
    dense_gate = jnp.dot(
        tokens,
        lax.all_gather(w_dense_gate, tok_axes, axis=0, tiled=True),
        preferred_element_type=jnp.float32,
    )
    dense_up = jnp.dot(
        tokens,
        lax.all_gather(w_dense_up, tok_axes, axis=0, tiled=True),
        preferred_element_type=jnp.float32,
    )
    dense_hidden = (jax.nn.silu(dense_gate) * dense_up).astype(jnp.bfloat16)
    dense_part = jnp.dot(
        dense_hidden,
        lax.all_gather(w_dense_down, tok_axes, axis=1, tiled=True),
        preferred_element_type=jnp.float32,
    )
    dense = lax.psum_scatter(
        dense_part.astype(jnp.bfloat16), "dp", scatter_dimension=1, tiled=True
    )
    return (dense.astype(jnp.float32) + weighted).astype(jnp.bfloat16)


def solution(mesh):
    n_dp, n_expert = mesh.devices.shape
    fine = Mesh(mesh.devices.reshape(n_dp, n_expert // 2, 2), ("dp", "group", "core"))
    ex = ("group", "core")
    in_specs = (
        P(ex, None),
        P(ex, None),
        P(ex, None),
        P(ex, "dp"),
        P(ex, "dp"),
        P("dp", ex),
        P("dp", ex, None, None),
        P("dp", ex, None, None),
        P("dp", ex, None, None),
    )
    return jax.shard_map(
        per_device, mesh=fine, in_specs=in_specs, out_specs=P(ex, "dp"), check_vma=False
    )
```

time: 987 us -> 699 us (0.71)
  blocking collectives: 337 us -> 47.3 us
  waiting for transfers between devices: 565 us -> 594 us
  local copies, waits for them, and re-layouts: 28.6 us -> 5.44 us
    all_to_all x1, blocking collectives: 337 us -> 47.3 us  [per_device(): lax.all_to_all(outgoing, ('group', 'core'), split_axis=0, concat_axis=0,...]
    all_to_all x1, waiting for transfers between devices: 120 us -> 30.8 us  [per_device(): lax.all_to_all(summed, ('group', 'core'), split_axis=0, concat_axis=0, ti...]
    reduce_scatter x1 -> x2, waiting for transfers between devices: 83.5 us -> 144 us  [the longest x1 100 us: per_device(): lax.psum_scatter(result, ('dp', 'core'), scatter_dimension=1, tiled=True)]
    all_gather x3 -> x4, waiting for transfers between devices: 359 us -> 417 us  [the longest x1 122 us: per_device(): lax.all_gather(w_dense_down, tok_axes, axis=1, tiled=True)]
    convert_element_type x3 -> x0, local copies, waits for them, and re-layouts: 10.5 us -> none  [the longest x1 5.78 us: per_device(): result.astype(jnp.bfloat16)]
    dot_general x7 -> x6, matrix products: 22.9 us -> 23.3 us  [the longest x1 7.77 us: per_device(): jnp.dot(hidden, w_exp_down[0, 0], preferred_element_type=jnp.float32)]
  transfers between devices with their start and end apart: 5 -> 7, of which waited for: 5 -> 7; matrix products, arithmetic and copies ran while one was open for 2% -> 3% of each run, Pallas kernels for 0% -> 0%
where the time goes in v1:
time: 699 us
  waiting for transfers between devices  594 us (85%)
  blocking collectives  47.3 us (7%)
  matrix products  23.3 us (3%)
  between operations  13.6 us (2%)
  starting transfers between devices  13.4 us (2%)
    all_gather x1, waiting for transfers between devices, per_device(): lax.all_gather(w_dense_down, tok_axes, axis=1, tiled=True)  122 us
    all_gather x1, waiting for transfers between devices, per_device(): lax.all_gather(w_dense_up, tok_axes, axis=0, tiled=True)  119 us
    all_gather x1, waiting for transfers between devices, per_device(): lax.all_gather(w_dense_gate, tok_axes, axis=0, tiled=True)  112 us
    reduce_scatter x1, waiting for transfers between devices, per_device(): lax.psum_scatter(result, ('dp', 'core'), scatter_dimension=1, tiled=True)  100 us
    all_gather x1, waiting for transfers between devices, per_device(): allcols = lax.all_gather(rows, ('dp', 'core'), axis=0, tiled=False)  64.9 us
    all_to_all x1, blocking collectives, per_device(): lax.all_to_all(outgoing, ('group', 'core'), split_axis=0, concat_axis=0,...  47.3 us
    reduce_scatter x1, waiting for transfers between devices, per_device(): lax.psum_scatter(dense_part.astype(jnp.bfloat16), 'dp', scatter_dimension...  43.6 us
    all_to_all x1, waiting for transfers between devices, per_device(): lax.all_to_all(summed, ('group', 'core'), split_axis=0, concat_axis=0, ti...  30.8 us
  transfers between devices with their start and end apart: 7, of which 7 were waited for; matrix products, arithmetic and copies ran while one was open for 3% of the time, Pallas kernels for 0%

profile of v1, /device:TPU:32, one launch (start us, length us, event | category | flops | bytes accessed | tf_op | source)
XLA Modules:
  0.0 698.7 jit_solution(16514132305830025764)
XLA Ops:
  6.5 0.9 copy.45
  7.4 0.1 eq.43
  7.6 0.1 eq.39
  7.7 0.6 reduce-window.6
  8.3 0.2 slice_reduce_fusion
  8.6 0.1 reduce_sum.33
  8.9 0.7 multiply_add_fusion
  9.6 1.2 convolution_convert_fusion.2
  10.8 0.2 reshape.55
  11.2 47.3 %all_to_all.10 = bf16[64,10,224]{2,1,0:T(8,128)(2,1)S(1)} all-to-all(bf16[64,10,224]{2,1,0:T(8,128)(2,1)S(1)} %bitcast.50), channel_id=1, replica_groups=mesh['dp'=8,'group'=32,'core'=2] {'group','core'}, dimensions={0} | all-to-all | bytes 573440 | tf_op jit(solution)/shard_map/all_to_all | solution.py:43
  58.5 0.2 all_gather_reshape.3
  58.7 0.9 copy.51
  59.6 0.7 all-gather.5.cloned.1.call-update
  60.4 0.7 all-gather.7.cloned.1.call-update
  61.1 0.5 all-gather.9.cloned.1.call-update
  61.7 64.9 %all-gather.11.cloned.1.call-done = bf16[16,640,224]{1,2,0:T(8,128)(2,1)} async-done(((bf16[1,640,224]{1,2,0:T(8,128)(2,1)}), bf16[16,640,224]{1,2,0:T(8,128)(2,1)}) %all-gather.11.cloned.1.call-update) | async-done | bytes 4587536 | tf_op jit(solution)/shard_map/all_gather | solution.py:45
  126.6 3.3 fusion.6
  130.0 7.8 %convolution_convert_fusion = bf16[640,3584]{0,1:T(8,128)(2,1)} fusion(bf16[640,3584]{0,1:T(8,128)(2,1)} %bitcast.54, bf16[1,1,152,3584]{3,2,1,0:T(8,128)(2,1)S(1)} %copy-done, bf16[1,1,3584,152]{2,3,1,0:T(8,128)(2,1)} %param.16, f32[640,152]{0,1:T(8,128)S(1)} %fusion.6), kind=kOutput, calls=%fused_computation | convolution fusion | flops 1397483520 | bytes 11743232 | tf_op jit(solution)/shard_map/dot_general | solution.py:51
  137.8 112.2 %all-gather.5.cloned.1.call-done = bf16[3584,304]{1,0:T(8,128)(2,1)} async-done(((bf16[56,304]{1,0:T(8,128)(2,1)}), bf16[3584,304]{1,0:T(8,128)(2,1)}) %all-gather.5.cloned.1.call-update) | async-done | bytes 2179088 | tf_op jit(solution)/shard_map/all_gather | solution.py:63
  250.0 2.9 fusion.30
  252.9 118.8 %all-gather.7.cloned.1.call-done = bf16[3584,304]{1,0:T(8,128)(2,1)} async-done(((bf16[56,304]{1,0:T(8,128)(2,1)}), bf16[3584,304]{1,0:T(8,128)(2,1)}) %all-gather.7.cloned.1.call-update) | async-done | bytes 2179088 | tf_op jit(solution)/shard_map/all_gather | solution.py:68
  371.7 121.6 %all-gather.9.cloned.1.call-done = bf16[304,3584]{0,1:T(8,128)(2,1)} async-done(((bf16[304,56]{0,1:T(8,128)(2,1)}), bf16[304,3584]{0,1:T(8,128)(2,1)}) %all-gather.9.cloned.1.call-update) | async-done | bytes 2179088 | tf_op jit(solution)/shard_map/all_gather | solution.py:74
  493.3 6.2 convolution_convert_fusion.1
  499.6 100.3 %reduce-scatter.5.cloned.1.call-done = bf16[640,224]{0,1:T(8,128)(2,1)} async-done(((bf16[640,3584]{0,1:T(8,128)(2,1)}), bf16[640,224]{0,1:T(8,128)(2,1)}) %reduce-scatter.5.cloned.1.call-update) | async-done | bytes 286736 | tf_op jit(solution)/shard_map/reduce_scatter | solution.py:53
  599.8 1.1 copy.52
  601.0 0.9 reshape.58
  601.9 13.2 %all-to-all-start.1 = ((bf16[64,10,224]{2,1,0:T(8,128)(2,1)}), bf16[64,10,224]{2,1,0:T(8,128)(2,1)S(1)}, u32[]{:S(2)}, u32[]{:S(2)}) async-start(bf16[64,10,224]{2,1,0:T(8,128)(2,1)} %reshape.58), calls=%async_computation.3 | async-start | bytes 1048576 | tf_op jit(solution)/shard_map/all_to_all | solution.py:55
  615.2 30.8 %all-to-all-done.1 = bf16[64,10,224]{2,1,0:T(8,128)(2,1)S(1)} async-done(((bf16[64,10,224]{2,1,0:T(8,128)(2,1)}), bf16[64,10,224]{2,1,0:T(8,128)(2,1)S(1)}, u32[]{:S(2)}, u32[]{:S(2)}) %all-to-all-start.1) | async-done | bytes 286752 | tf_op jit(solution)/shard_map/all_to_all | solution.py:55
  646.0 0.3 copy.59
  646.2 0.2 reshape.60
  646.4 43.6 %reduce-scatter.3.cloned.1.call-done = bf16[128,448]{0,1:T(8,128)(2,1)} async-done(((bf16[128,3584]{0,1:T(8,128)(2,1)}), bf16[128,448]{0,1:T(8,128)(2,1)}) %reduce-scatter.3.cloned.1.call-update) | async-done | bytes 114704 | tf_op jit(solution)/shard_map/reduce_scatter | solution.py:77
  690.0 1.9 fusion.1
  (25 shorter events, 0.6 us)
Async XLA Ops:
  6.5 123.4 %copy-start = (bf16[1,1,152,3584]{3,2,1,0:T(8,128)(2,1)S(1)}, bf16[1,1,152,3584]{3,2,1,0:T(8,128)(2,1)}, u32[]{:S(2)}) copy-start(bf16[1,1,152,3584]{3,2,1,0:T(8,128)(2,1)} %param.17) | copy-start | bytes 3268612
  6.5 120.1 %all-gather.11.cloned.1.call-start = ((), (), s32[]{:S(2)}) async-start(), calls=%async_computation.8 | async-start | bytes 4874240 | tf_op jit(solution)/shard_map/all_gather | solution.py:45
  7.4 119.2 %copy-start.3 = (bf16[1,1,3584,152]{2,3,1,0:T(8,128)(2,1)S(1)}, bf16[1,1,3584,152]{2,3,1,0:T(8,128)(2,1)}, u32[]{:S(2)}) copy-start(bf16[1,1,3584,152]{2,3,1,0:T(8,128)(2,1)} %param.15) | copy-start | bytes 3268612
  59.6 190.4 %all-gather.5.cloned.1.call-start = ((), (), s32[]{:S(2)}) async-start(), calls=%async_computation.4 | async-start | bytes 2795520 | tf_op jit(solution)/shard_map/all_gather | solution.py:63
  60.3 311.4 %all-gather.7.cloned.1.call-start = ((), (), s32[]{:S(2)}) async-start(), calls=%async_computation.5 | async-start | bytes 2795520 | tf_op jit(solution)/shard_map/all_gather | solution.py:68
  61.1 432.2 %all-gather.9.cloned.1.call-start = ((), (), s32[]{:S(2)}) async-start(), calls=%async_computation.6 | async-start | bytes 2795520 | tf_op jit(solution)/shard_map/all_gather | solution.py:74
  61.6 538.2 %reduce-scatter.5.cloned.1.call-start = ((), (), s32[]{:S(2)}) async-start(), calls=%async_computation.9 | async-start | bytes 4874240 | tf_op jit(solution)/shard_map/reduce_scatter | solution.py:53
  137.8 112.3 %copy-start.1 = (bf16[128,3584]{1,0:T(8,128)(2,1)S(1)}, bf16[128,3584]{1,0:T(8,128)(2,1)}, u32[]{:S(2)}) copy-start(bf16[128,3584]{1,0:T(8,128)(2,1)} %param.9) | copy-start | bytes 2752516
  137.8 552.2 %reduce-scatter.3.cloned.1.call-start = ((), (), s32[]{:S(2)}) async-start(), calls=%async_computation.7 | async-start | bytes 1032192 | tf_op jit(solution)/shard_map/reduce_scatter | solution.py:77
  499.5 115.6 %copy-start.2 = (f32[128,2]{0,1:T(2,128)S(1)}, f32[128,2]{0,1:T(2,128)}, u32[]{:S(2)}) copy-start(f32[128,2]{0,1:T(2,128)} %param.11) | copy-start | bytes 3076
  601.9 44.1 %all-to-all-start.1 = ((bf16[64,10,224]{2,1,0:T(8,128)(2,1)}), bf16[64,10,224]{2,1,0:T(8,128)(2,1)S(1)}, u32[]{:S(2)}, u32[]{:S(2)}) async-start(bf16[64,10,224]{2,1,0:T(8,128)(2,1)} %reshape.58), calls=%async_computation.3 | async-start | bytes 1048576 | tf_op jit(solution)/shard_map/all_to_all | solution.py:55
Sparse Core Ops, SparseCore 0:
  59.7 66.8 all-gather.10
  128.8 121.2 all-gather.4
  252.2 119.5 all-gather.6
  373.7 119.5 all-gather.8
  498.1 101.6 reduce-scatter.4
  604.1 85.8 reduce-scatter.2

commit v2 on v0

v2 whole, which is shorter than its diff:
```python
import functools

import jax
import jax.numpy as jnp
from jax import lax
from jax.experimental import pallas as pl
from jax.experimental.pallas import tpu as pltpu
from jax.sharding import PartitionSpec as P

CAP = 10
SLOT = 16
NZ = 16
NY = 4
NDP = 8
NT = 128
D = 3584
HH = 152
BLOCK = 8 * CAP
CHIP_ROWS = 112
COLS = 448
CHUNK = 512
MESH = pl.DeviceIdType.MESH
F32 = jnp.float32
BF16 = jnp.bfloat16


def dz_of(j, xl_to, i):
    d = jnp.where(xl_to == 0, j, 8 - j)
    edge = (d % 8) == 0
    first = jnp.where(edge, 0, d)
    second = jnp.where(edge, 8, NZ - d)
    return jnp.where(i == 0, first, second)


def kernel(
    routes, routes_t, weights, tok_hbm, pack_hbm, wg_hbm, wu_hbm, wd_hbm, out,
    tok2, sbuf, rbuf, xbuf, obuf, rsum, tbuf, ret, wg, wu, wd, mine, theirs, dense_w,
    d_mine, d_send, d_recv, term, fin,
    loc, core_send, core_recv, dis_send, dis_recv, bc_send, bc_recv,
    right_send, right_recv, left_send, left_recv, x_send, x_recv,
    rs_send, rs_recv, ret_send, ret_recv, fin_send, fin_recv,
):
    b = lax.axis_index("dp")
    ex = lax.axis_index("expert")
    core = ex % 2
    chip = ex // 2
    z = chip % NZ
    xl = chip // NZ
    y = b // 2
    active = (b % 2) == core
    j_me = (b + 15 - core) % 8

    def dev(bb, xx, zz, cc):
        return (bb, (xx * NZ + zz) * 2 + cc)

    def remote(src, dst, send, recv, to):
        return pltpu.make_async_remote_copy(
            src_ref=src, dst_ref=dst, send_sem=send, recv_sem=recv, device_id=to,
            device_id_type=MESH,
        )

    def dest_of(k):
        to_x, i = k // 2, k % 2
        return to_x, (z + dz_of(j_me, to_x, i)) % NZ

    def source_of(slot):
        i, s_x, s_c = slot // 4, (slot // 2) % 2, slot % 2
        j = (b + 15 - s_c) % 8
        return s_x, (z + NZ - dz_of(j, xl, i)) % NZ, s_c

    local = [
        pltpu.make_async_copy(tok_hbm, tok2.at[pl.ds(0, NT)], loc.at[0]),
        pltpu.make_async_copy(pack_hbm.at[core], mine, loc.at[1]),
        pltpu.make_async_copy(wg_hbm, wg.at[0], loc.at[2]),
        pltpu.make_async_copy(wu_hbm, wu.at[0], loc.at[3]),
        pltpu.make_async_copy(wd_hbm, wd.at[0], loc.at[4]),
    ]
    for copy in local:
        copy.start()

    barrier = pltpu.get_barrier_semaphore()

    def greet(to):
        pl.semaphore_signal(barrier, inc=1, device_id=to, device_id_type=MESH)

    @pl.loop(1, NDP)
    def _(k):
        greet(((b + k) % NDP, ex))

    partner = (b, chip * 2 + 1 - core)
    across = dev(b, 1 - xl, z, core)
    up_z = dev(b, xl, (z + 1) % NZ, core)
    down_z = dev(b, xl, (z + NZ - 1) % NZ, core)
    for to in (partner, across, up_z, down_z):
        greet(to)

    @pl.loop(0, 4)
    def _(k):
        to_x, to_z = dest_of(k)
        greet(dev(b, to_x, to_z, b % 2))

    @pl.when(active)
    def _():
        @pl.loop(0, 8)
        def _(s):
            s_x, s_z, s_c = source_of(s)
            greet(dev(b, s_x, s_z, s_c))

    pl.semaphore_wait(barrier, jnp.where(active, 7 + 4 + 4 + 8, 7 + 4 + 4))

    to_partner = [
        remote(pack_hbm.at[1 - core], theirs, core_send.at[0], core_recv.at[0], partner),
        remote(wg_hbm, wg.at[1], core_send.at[1], core_recv.at[1], partner),
        remote(wu_hbm, wu.at[1], core_send.at[2], core_recv.at[2], partner),
        remote(wd_hbm, wd.at[1], core_send.at[3], core_recv.at[3], partner),
        remote(tok_hbm, tok2.at[pl.ds(NT, NT)], core_send.at[4], core_recv.at[4], partner),
    ]
    for copy in to_partner:
        copy.start()

    row = lax.broadcasted_iota(jnp.int32, (4 * SLOT, NT), 0)
    k_row = row // SLOT
    e_row = (k_row // 2) * NZ + (z + dz_of(j_me, k_row // 2, k_row % 2)) % NZ
    hit = (routes_t[0:1, :] == e_row) | (routes_t[1:2, :] == e_row)
    before = (
        lax.broadcasted_iota(jnp.int32, (NT, NT), 0)
        < lax.broadcasted_iota(jnp.int32, (NT, NT), 1)
    )
    rank = jnp.dot(
        jnp.where(hit, 1.0, 0.0).astype(BF16),
        jnp.where(before, 1.0, 0.0).astype(BF16),
        preferred_element_type=F32,
    )
    select = jnp.where(hit & (rank == (row % SLOT).astype(F32)), 1.0, 0.0).astype(BF16)
    local[0].wait()
    for n in range(D // CHUNK):
        cols = pl.ds(n * CHUNK, CHUNK)
        sbuf[:, cols] = jnp.dot(
            select, tok2[0:NT, cols], preferred_element_type=F32
        ).astype(BF16)

    def dispatch(k):
        to_x, to_z = dest_of(k)
        slot = (k % 2) * 4 + xl * 2 + core
        return remote(
            sbuf.at[pl.ds(pl.multiple_of(k * SLOT, SLOT), SLOT)],
            rbuf.at[pl.ds(pl.multiple_of(slot * SLOT, SLOT), SLOT)],
            dis_send.at[k], dis_recv.at[slot], dev(b, to_x, to_z, b % 2),
        )

    @pl.loop(0, 4)
    def _(k):
        dispatch(k).start()

    local[1].wait()
    to_partner[0].wait_recv()

    def shard(xx, zz):
        start = (xx * NZ + zz) * CHIP_ROWS
        return dense_w.at[pl.ds(pl.multiple_of(start, 16), CHIP_ROWS)]

    first = jnp.where(core == 0, mine[...], theirs[...])
    second = jnp.where(core == 0, theirs[...], mine[...])
    dense_w[pl.ds(pl.multiple_of(chip * CHIP_ROWS, 16), CHIP_ROWS), :] = jnp.concatenate(
        [first, second], axis=0
    )

    slot_row = lax.broadcasted_iota(jnp.int32, (BLOCK, 8 * SLOT), 0)
    slot_col = lax.broadcasted_iota(jnp.int32, (BLOCK, 8 * SLOT), 1)
    squeeze = jnp.where(
        slot_col == (slot_row // CAP) * SLOT + slot_row % CAP, 1.0, 0.0
    ).astype(BF16)

    def spread(k):
        return remote(
            xbuf.at[y], xbuf.at[y], bc_send.at[k - 1], bc_recv.at[y], ((b + k) % NDP, ex)
        )

    @pl.when(active)
    def _():
        @pl.loop(0, 8)
        def _(s):
            remote(
                sbuf.at[pl.ds(0, SLOT)],
                rbuf.at[pl.ds(pl.multiple_of(s * SLOT, SLOT), SLOT)],
                dis_send.at[0], dis_recv.at[s], partner,
            ).wait_recv()

        for n in range(D // CHUNK):
            cols = pl.ds(n * CHUNK, CHUNK)
            xbuf[y, :, cols] = jnp.dot(
                squeeze, rbuf[:, cols], preferred_element_type=F32
            ).astype(BF16)

        @pl.loop(1, NDP)
        def _(k):
            spread(k).start()

    def go_right(k):
        s = shard(xl, (z + NZ - k) % NZ)
        return remote(s, s, right_send.at[k], right_recv.at[k], up_z)

    def go_left(k):
        s = shard(xl, (z + k) % NZ)
        return remote(s, s, left_send.at[k], left_recv.at[k], down_z)

    def go_across(k):
        s = shard(xl, (z + k) % NZ)
        return remote(s, s, x_send.at[k], x_recv.at[k], across)

    go_right(0).start()
    go_left(0).start()
    go_across(0).start()

    @pl.loop(1, 8)
    def _(k):
        go_right(k - 1).wait_recv()
        go_right(k).start()
        go_left(k - 1).wait_recv()

        @pl.when(k < 7)
        def _():
            go_left(k).start()

        go_across(NZ - k).start()
        go_across(k).start()

    go_right(7).wait_recv()
    go_across(8).start()

    for copy in local[2:]:
        copy.wait()
    for copy in to_partner[1:4]:
        copy.wait_recv()

    def back(yy):
        return remote(
            obuf.at[yy], rsum.at[b], rs_send.at[yy], rs_recv.at[b], (2 * yy + core, ex)
        )

    @pl.loop(0, NY)
    def _(k):
        yy = (y + k) % NY
        foreign = jnp.logical_not(active & (k == 0))

        @pl.when(foreign)
        def _():
            remote(
                xbuf.at[yy], xbuf.at[yy], bc_send.at[0], bc_recv.at[yy], partner
            ).wait_recv()

        x = xbuf[yy]
        hidden = []
        for h in range(2):
            gate = jnp.dot(x, wg[h], preferred_element_type=F32)
            up = jnp.dot(x, wu[h], preferred_element_type=F32)
            hidden.append((gate / (1.0 + jnp.exp(-gate)) * up).astype(BF16))
        for n in range(D // CHUNK):
            cols = pl.ds(n * CHUNK, CHUNK)
            obuf[yy, :, cols] = (
                jnp.dot(hidden[0], wd[0, :, cols], preferred_element_type=F32)
                + jnp.dot(hidden[1], wd[1, :, cols], preferred_element_type=F32)
            ).astype(BF16)

        @pl.when(foreign)
        def _():
            back(yy).start()

    to_partner[4].wait_recv()

    @pl.loop(0, NZ)
    def _(k):
        s = shard(1 - xl, (z + k) % NZ)
        remote(s, s, x_send.at[k], x_recv.at[k], across).wait_recv()

    both = jnp.dot(tok2[...], dense_w[:, 0:384], preferred_element_type=F32)
    ups = pltpu.roll(both, 384 - HH, 1)
    dense_hidden = both / (1.0 + jnp.exp(-both)) * ups
    lane = lax.broadcasted_iota(jnp.int32, (2 * NT, 384), 1)
    dense_hidden = jnp.where(lane < HH, dense_hidden, 0.0)
    placed = pltpu.roll(dense_hidden, 2 * HH - 256, 1)[:, 0:256].astype(BF16)
    for n in range(D // CHUNK):
        part = lax.dot_general(
            placed,
            dense_w[n * CHUNK:(n + 1) * CHUNK, 256:512],
            (((1,), (1,)), ((), ())),
            preferred_element_type=F32,
        )
        cols = pl.ds(n * CHUNK, CHUNK)
        d_mine[:, cols] = part[0:NT]
        d_send[:, cols] = part[NT:2 * NT].astype(BF16)
    swap = remote(d_send, d_recv, core_send.at[5], core_recv.at[5], partner)
    swap.start()

    def give(s):
        s_x, s_z, s_c = source_of(s)
        k = xl * 2 + s // 4
        return remote(
            tbuf.at[pl.ds(pl.multiple_of(s * SLOT, SLOT), SLOT)],
            ret.at[pl.ds(pl.multiple_of(k * SLOT, SLOT), SLOT)],
            ret_send.at[s], ret_recv.at[k], dev(b, s_x, s_z, s_c),
        )

    @pl.when(active)
    def _():
        @pl.loop(1, NDP)
        def _(k):
            src = (b + k) % NDP
            remote(
                obuf.at[0], rsum.at[src], rs_send.at[0], rs_recv.at[src], partner
            ).wait_recv()

        widen = jnp.where(
            lax.broadcasted_iota(jnp.int32, (8 * SLOT, BLOCK), 0)
            == (lax.broadcasted_iota(jnp.int32, (8 * SLOT, BLOCK), 1) // CAP) * SLOT
            + lax.broadcasted_iota(jnp.int32, (8 * SLOT, BLOCK), 1) % CAP,
            1.0, 0.0,
        ).astype(BF16)
        for n in range(D // CHUNK):
            cols = pl.ds(n * CHUNK, CHUNK)
            total = obuf[y, :, cols].astype(F32)
            for k in range(1, NDP):
                total = total + rsum[(b + k) % NDP, :, cols].astype(F32)
            tbuf[:, cols] = jnp.dot(
                widen, total.astype(BF16), preferred_element_type=F32
            ).astype(BF16)

        @pl.loop(0, 8)
        def _(s):
            give(s).start()

    col = lax.broadcasted_iota(jnp.int32, (NT, 4 * SLOT), 1)
    k_col = col // SLOT
    e_col = (k_col // 2) * NZ + (z + dz_of(j_me, k_col // 2, k_col % 2)) % NZ
    hit0 = routes[:, 0:1] == e_col
    hit1 = routes[:, 1:2] == e_col
    earlier = (
        lax.broadcasted_iota(jnp.int32, (NT, NT), 1)
        < lax.broadcasted_iota(jnp.int32, (NT, NT), 0)
    )
    rank_col = jnp.dot(
        jnp.where(earlier, 1.0, 0.0).astype(BF16),
        jnp.where(hit0 | hit1, 1.0, 0.0).astype(BF16),
        preferred_element_type=F32,
    )
    share = jnp.where(hit0, weights[:, 0:1], 0.0) + jnp.where(hit1, weights[:, 1:2], 0.0)
    share = jnp.where(rank_col == (col % SLOT).astype(F32), share, 0.0)
    share_hi = share.astype(BF16)
    share_lo = (share - share_hi.astype(F32)).astype(BF16)

    swap.wait_recv()

    @pl.loop(0, 4)
    def _(k):
        remote(
            tbuf.at[pl.ds(0, SLOT)],
            ret.at[pl.ds(pl.multiple_of(k * SLOT, SLOT), SLOT)],
            ret_send.at[0], ret_recv.at[k], partner,
        ).wait_recv()

    for n in range(NDP // 2):
        cols = pl.ds(n * 2 * COLS, 2 * COLS)
        rows = ret[:, cols]
        value = (
            d_mine[:, cols]
            + d_recv[:, cols].astype(F32)
            + jnp.dot(share_hi, rows, preferred_element_type=F32)
            + jnp.dot(share_lo, rows, preferred_element_type=F32)
        ).astype(BF16)
        term[2 * n] = value[:, 0:COLS]
        term[2 * n + 1] = value[:, COLS:2 * COLS]

    def finish(k):
        to = (b + k) % NDP
        return remote(
            term.at[to], fin.at[b], fin_send.at[k - 1], fin_recv.at[b], (to, ex)
        )

    @pl.loop(1, NDP)
    def _(k):
        finish(k).start()

    @pl.loop(1, NDP)
    def _(k):
        src = (b + k) % NDP
        remote(
            term.at[0], fin.at[src], fin_send.at[0], fin_recv.at[src], partner
        ).wait_recv()

    total = term[b].astype(F32)
    for k in range(1, NDP):
        total = total + fin[(b + k) % NDP].astype(F32)
    out[...] = total.astype(BF16)

    for copy in to_partner:
        copy.wait_send()
    swap.wait_send()

    @pl.loop(0, 4)
    def _(k):
        dispatch(k).wait_send()

    @pl.loop(0, 8)
    def _(k):
        go_right(k).wait_send()

    @pl.loop(0, 7)
    def _(k):
        go_left(k).wait_send()

    @pl.loop(0, NZ)
    def _(k):
        go_across(k).wait_send()

    @pl.loop(0, NY)
    def _(k):
        @pl.when(jnp.logical_not(active & (k == 0)))
        def _():
            back((y + k) % NY).wait_send()

    @pl.when(active)
    def _():
        @pl.loop(1, NDP)
        def _(k):
            spread(k).wait_send()

        @pl.loop(0, 8)
        def _(s):
            give(s).wait_send()

    @pl.loop(1, NDP)
    def _(k):
        finish(k).wait_send()


def per_device(
    tokens, routes, gate_weights, w_dense_gate, w_dense_up, w_dense_down,
    w_exp_gate, w_exp_up, w_exp_down,
):
    down_t = w_dense_down.T
    pad = jnp.zeros((w_dense_gate.shape[0], CHUNK - 3 * HH), BF16)
    pack = jnp.stack(
        [
            jnp.concatenate(
                [w[:, h * HH:(h + 1) * HH] for w in (w_dense_gate, w_dense_up, down_t)] + [pad],
                axis=1,
            )
            for h in range(2)
        ]
    )
    rows = w_dense_gate.shape[0]
    vmem = pl.BlockSpec(memory_space=pltpu.VMEM)
    hbm = pl.BlockSpec(memory_space=pl.ANY)
    dma = pltpu.SemaphoreType.DMA
    return pl.pallas_call(
        kernel,
        out_shape=jax.ShapeDtypeStruct((NT, COLS), BF16),
        in_specs=[vmem, vmem, vmem, hbm, hbm, hbm, hbm, hbm],
        out_specs=vmem,
        scratch_shapes=[
            pltpu.VMEM((2 * NT, D), BF16),
            pltpu.VMEM((4 * SLOT, D), BF16),
            pltpu.VMEM((8 * SLOT, D), BF16),
            pltpu.VMEM((NY, BLOCK, D), BF16),
            pltpu.VMEM((NY, BLOCK, D), BF16),
            pltpu.VMEM((NDP, BLOCK, D), BF16),
            pltpu.VMEM((8 * SLOT, D), BF16),
            pltpu.VMEM((4 * SLOT, D), BF16),
            pltpu.VMEM((2, D, HH), BF16),
            pltpu.VMEM((2, D, HH), BF16),
            pltpu.VMEM((2, HH, D), BF16),
            pltpu.VMEM((rows, CHUNK), BF16),
            pltpu.VMEM((rows, CHUNK), BF16),
            pltpu.VMEM((D, CHUNK), BF16),
            pltpu.VMEM((NT, D), F32),
            pltpu.VMEM((NT, D), BF16),
            pltpu.VMEM((NT, D), BF16),
            pltpu.VMEM((NDP, NT, COLS), BF16),
            pltpu.VMEM((NDP, NT, COLS), BF16),
            dma((5,)), dma((6,)), dma((6,)), dma((4,)), dma((8,)), dma((7,)), dma((4,)),
            dma((8,)), dma((8,)), dma((7,)), dma((7,)), dma((16,)), dma((16,)),
            dma((4,)), dma((8,)), dma((8,)), dma((4,)), dma((7,)), dma((8,)),
        ],
        compiler_params=pltpu.CompilerParams(
            collective_id=0, has_side_effects=True, vmem_limit_bytes=56 * 1024 * 1024
        ),
    )(
        routes, routes.T, gate_weights, tokens, pack,
        w_exp_gate[0, 0], w_exp_up[0, 0], w_exp_down[0, 0],
    )


def solution(mesh):
    in_specs = (
        P("expert", None),
        P("expert", None),
        P("expert", None),
        P("expert", "dp"),
        P("expert", "dp"),
        P("dp", "expert"),
        P("dp", "expert", None, None),
        P("dp", "expert", None, None),
        P("dp", "expert", None, None),
    )
    return jax.shard_map(
        per_device, mesh=mesh, in_specs=in_specs, out_specs=P("expert", "dp"), check_vma=False
    )
```

time: 987 us -> 194 us (0.20)
  the two profiles are of different devices: /device:TPU:32 before, /device:TPU:43 now
where the time goes in v2:
time: 194 us
  Pallas kernels  182 us (94%)
  local copies, waits for them, and re-layouts  10.7 us (6%)
    pallas_call x1, Pallas kernels, per_device(): pl.pallas_call(kernel, out_shape=jax.ShapeDtypeStruct((NT, COLS), BF16),...  182 us
    unnamed x6, local copies, waits for them, and re-layouts  7.18 us

profile of v2, /device:TPU:43, one launch (start us, length us, event | category | flops | bytes accessed | tf_op | source)
XLA Modules:
  0.0 193.8 jit_solution(4657838127580643541)
XLA Ops:
  0.0 0.1 pad.9.clone
  0.1 0.9 fusion.2
  1.0 1.4 copy.13.weights
  2.4 1.4 copy.12.routes
  3.8 0.9 fusion
  4.7 0.1 maximum_bitcast_fusion
  4.8 0.7 pad_maximum_fusion.pack_hbm
  5.5 0.0 copy-start
  5.5 2.7 %copy.10 = bf16[1,1,3584,152]{3,2,1,0:T(8,128)(2,1)} copy(bf16[1,1,3584,152]{2,3,1,0:T(8,128)(2,1)} %param.15) | data formatting | bytes 2179072 | tf_op args[6]
  8.2 0.0 copy-done
  8.2 1.7 copy.11
  9.9 182.3 %shard_map.91 = bf16[128,448]{1,0:T(8,128)(2,1)} custom-call(s32[128,2]{1,0:T(8,128)} %copy.12.routes, s32[2,128]{1,0:T(2,128)} %bitcast.13, f32[128,2]{1,0:T(8,128)} %copy.13.weights, bf16[128,3584]{1,0:T(8,128)(2,1)} %tok_hbm.1, bf16[2,56,512]{2,1,0:T(8,128)(2,1)} %pad_maximum_fusion.pack_hbm, bf16[3584,152]{1,0:T(8,128)(2,1)} %bitcast.9, ...), custom_call_target="tpu_custom_call" | custom-call | tf_op jit(solution)/shard_map/pallas_call | solution.py:455
  192.2 1.7 copy.14
  (1 shorter events, 0.0 us)
Async XLA Ops:
  5.5 2.7 %copy-start = (bf16[1,1,3584,152]{2,3,1,0:T(8,128)(2,1)S(1)}, bf16[1,1,3584,152]{2,3,1,0:T(8,128)(2,1)}, u32[]{:S(2)}) copy-start(bf16[1,1,3584,152]{2,3,1,0:T(8,128)(2,1)} %param.16) | copy-start | bytes 3268612

commit v3 on v0

v3 whole, which is shorter than its diff:
```python
import jax
import jax.numpy as jnp
from jax import lax
from jax.experimental import pallas as pl
from jax.experimental.pallas import tpu as pltpu
from jax.sharding import PartitionSpec as P

CAP = 10
SLOT = 16
NZ = 16
NY = 4
NDP = 8
NT = 128
D = 3584
HALF = D // 2
HH = 152
BLOCK = 8 * CAP
CHIP_ROWS = 112
COLS = 448
CHUNK = 512
PIECE = 256
EXPERTS = 32
MESH = pl.DeviceIdType.MESH
F32 = jnp.float32
BF16 = jnp.bfloat16


def dz_of(j, xl_to, i):
    d = jnp.where(xl_to == 0, j, 8 - j)
    edge = (d % 8) == 0
    first = jnp.where(edge, 0, d)
    second = jnp.where(edge, 8, NZ - d)
    return jnp.where(i == 0, first, second)


def iota(shape, dim):
    return lax.broadcasted_iota(jnp.int32, shape, dim)


def ones_where(mask):
    return jnp.where(mask, 1.0, 0.0).astype(BF16)


def dot(a, b):
    return jnp.dot(a, b, preferred_element_type=F32)


def dot_nt(a, b):
    return lax.dot_general(a, b, (((1,), (1,)), ((), ())), preferred_element_type=F32)


def silu(v):
    return v / (1.0 + jnp.exp(-v))


def kernel(
    routes_t, weights_t, dg, du, dd_t, tok_hbm, wg_hbm, wu_hbm, wd_hbm, out,
    tok, tq, sbuf, rbuf, xbuf, obuf, rsum, tbuf, ret, wg, wu, wd, pack, theirs, dense_w,
    gu, gu_send, gu_recv, hbuf, d_mine, d_send, d_recv, dterm, fin,
    loc, core_send, core_recv, ac_send, ac_recv, dis_send, dis_recv, bc_send, bc_recv,
    right_send, right_recv, left_send, left_recv,
    rs_send, rs_recv, ret_send, ret_recv, fin_send, fin_recv,
):
    b = lax.axis_index("dp")
    ex = lax.axis_index("expert")
    core = ex % 2
    chip = ex // 2
    z = chip % NZ
    xl = chip // NZ
    y = b // 2
    active = (b % 2) == core
    own_half = (b // 4) == xl

    def dev(bb, xx, zz, cc):
        return (bb, (xx * NZ + zz) * 2 + cc)

    def remote(src, dst, send, recv, to):
        return pltpu.make_async_remote_copy(
            src_ref=src, dst_ref=dst, send_sem=send, recv_sem=recv, device_id=to,
            device_id_type=MESH,
        )

    def dest_of(bb, k):
        to_x, i = k // 2, k % 2
        return to_x, (z + dz_of((bb + 15 - core) % 8, to_x, i)) % NZ

    def source_of(bb, slot):
        i, s_x, s_c = slot // 4, (slot // 2) % 2, slot % 2
        return s_x, (z + NZ - dz_of((bb + 15 - s_c) % 8, xl, i)) % NZ, s_c

    def slab(ref, slot):
        return ref.at[pl.ds(pl.multiple_of(slot * SLOT, SLOT), SLOT)]

    def tok_half(which):
        return tok_hbm.at[:, pl.ds(pl.multiple_of(which * HALF, 128), HALF)]

    local = [
        pltpu.make_async_copy(tok_hbm, tok, loc.at[0]),
        pltpu.make_async_copy(wg_hbm, wg.at[0], loc.at[1]),
        pltpu.make_async_copy(wu_hbm, wu.at[0], loc.at[2]),
        pltpu.make_async_copy(wd_hbm, wd.at[0], loc.at[3]),
        pltpu.make_async_copy(tok_half(xl), tq.at[pl.ds(0, NT)], loc.at[4]),
    ]
    for copy in local:
        copy.start()

    barrier = pltpu.get_barrier_semaphore()

    def greet(to):
        pl.semaphore_signal(barrier, inc=1, device_id=to, device_id_type=MESH)

    partner = (b, chip * 2 + 1 - core)
    across = dev(b, 1 - xl, z, core)
    up_z = dev(b, xl, (z + 1) % NZ, core)
    down_z = dev(b, xl, (z + NZ - 1) % NZ, core)

    @pl.loop(1, NDP)
    def _(k):
        greet(((b + k) % NDP, ex))

    for to in (partner, across, up_z, down_z):
        greet(to)

    @pl.when(active)
    def _():
        @pl.loop(0, 8)
        def _(s):
            s_x, s_z, s_c = source_of(b, s)
            greet(dev(b, s_x, s_z, s_c))

    @pl.loop(0, EXPERTS)
    def _(n):
        bb = n // 4
        to_x, to_z = dest_of(bb, n % 4)
        greet(dev(b, to_x, to_z, bb % 2))

    @pl.loop(0, NDP)
    def _(k):
        @pl.when(jnp.logical_not(own_half & (k == b)))
        def _():
            greet(dev(k, b // 4, z, core))

    row = iota((4 * SLOT, NT), 0)
    k_row = row // SLOT
    e_row = (k_row // 2) * NZ + (z + dz_of((b + 15 - core) % 8, k_row // 2, k_row % 2)) % NZ
    hit = (routes_t[0:1, :] == e_row) | (routes_t[1:2, :] == e_row)
    before = ones_where(iota((NT, NT), 0) < iota((NT, NT), 1))
    rank = dot(ones_where(hit), before)
    select = ones_where(hit & (rank == (row % SLOT).astype(F32)))
    local[0].wait()
    for n in range(D // CHUNK):
        cols = pl.ds(n * CHUNK, CHUNK)
        sbuf[:, cols] = dot(select, tok[:, cols]).astype(BF16)

    hid = iota((2 * HH, CHUNK), 0)
    lane = iota((2 * HH, CHUNK), 1)
    for h in range(2):
        here = (hid >= h * HH) & (hid < (h + 1) * HH)
        total = None
        for n, part in enumerate((dg[...], du[...], dd_t[...])):
            placed = ones_where(here & (lane == hid - h * HH + n * HH))
            term = dot(part, placed)
            total = term if total is None else total + term
        pack[h] = total.astype(BF16)

    pl.semaphore_wait(
        barrier, jnp.where(own_half, 7, 8) + 7 + 4 + 4 + EXPERTS
    )

    def dispatch(h, k):
        to_x, to_z = dest_of(b, k)
        slot = (k % 2) * 4 + xl * 2 + core
        cols = pl.ds(pl.multiple_of(h * HALF, 128), HALF)
        return remote(
            slab(sbuf, k).at[:, cols], slab(rbuf, slot).at[:, cols],
            dis_send.at[h * 4 + k], dis_recv.at[h * 8 + slot], dev(b, to_x, to_z, b % 2),
        )

    @pl.loop(0, 8)
    def _(n):
        dispatch(n // 4, n % 4).start()

    to_partner = [
        remote(pack.at[1 - core], theirs, core_send.at[0], core_recv.at[0], partner),
        remote(tok_half(xl), tq.at[pl.ds(NT, NT)], core_send.at[1], core_recv.at[1], partner),
        remote(wg_hbm, wg.at[1], core_send.at[2], core_recv.at[2], partner),
        remote(wu_hbm, wu.at[1], core_send.at[3], core_recv.at[3], partner),
        remote(wd_hbm, wd.at[1], core_send.at[4], core_recv.at[4], partner),
    ]
    for copy in to_partner:
        copy.start()
    tok_across = remote(
        tok_half(1 - xl), tq.at[pl.ds(2 * NT, NT)], ac_send.at[0], ac_recv.at[0], across
    )
    tok_across.start()

    place = iota((EXPERTS * SLOT, NT), 0)
    hit0 = routes_t[0:1, :] == place // SLOT
    hit1 = routes_t[1:2, :] == place // SLOT
    rank_all = dot(ones_where(hit0 | hit1), before)
    share = jnp.where(hit0, weights_t[0:1, :], 0.0) + jnp.where(hit1, weights_t[1:2, :], 0.0)
    share = jnp.where(rank_all == (place % SLOT).astype(F32), share, 0.0).T
    share_hi = share.astype(BF16)
    share_lo = (share - share_hi.astype(F32)).astype(BF16)

    to_partner[0].wait_recv()
    mine = pack[core]
    first = jnp.where(core == 0, mine, theirs[...])
    second = jnp.where(core == 0, theirs[...], mine)
    dense_w[pl.ds(pl.multiple_of(z * CHIP_ROWS, 16), CHIP_ROWS), :] = jnp.concatenate(
        [first, second], axis=0
    )

    slot_row = iota((BLOCK, 8 * SLOT), 0)
    squeeze = ones_where(
        iota((BLOCK, 8 * SLOT), 1) == (slot_row // CAP) * SLOT + slot_row % CAP
    )

    def x_part(yy, h):
        return xbuf.at[yy, :, pl.ds(pl.multiple_of(h * HALF, 128), HALF)]

    def spread(h, k):
        return remote(
            x_part(y, h), x_part(y, h), bc_send.at[h * 7 + k - 1], bc_recv.at[h * 4 + y],
            ((b + k) % NDP, ex),
        )

    def wait_spread(yy, h):
        remote(
            x_part(yy, h), x_part(yy, h), bc_send.at[0], bc_recv.at[h * 4 + yy], partner
        ).wait_recv()

    @pl.when(active)
    def _():
        for h in range(2):
            cols = pl.ds(h * HALF, HALF)

            @pl.loop(0, 8)
            def _(s):
                remote(
                    slab(sbuf, 0).at[:, cols], slab(rbuf, s).at[:, cols],
                    dis_send.at[0], dis_recv.at[h * 8 + s], partner,
                ).wait_recv()

            xbuf[y, :, cols] = dot(squeeze, rbuf[:, cols]).astype(BF16)

            @pl.loop(1, NDP)
            def _(k):
                spread(h, k).start()

    tok_across.wait_recv()
    relay = remote(
        tq.at[pl.ds(2 * NT, NT)], tq.at[pl.ds(3 * NT, NT)], core_send.at[5], core_recv.at[5],
        partner,
    )
    relay.start()

    @pl.when(jnp.logical_not(active))
    def _():
        wait_spread(y, 0)

    def shard(zz, p):
        return dense_w.at[
            pl.ds(pl.multiple_of(zz * CHIP_ROWS, 16), CHIP_ROWS),
            pl.ds(p * PIECE, PIECE),
        ]

    def go_right(k, p):
        s = shard((z + NZ - k) % NZ, p)
        return remote(s, s, right_send.at[2 * k + p], right_recv.at[2 * k + p], up_z)

    def go_left(k, p):
        s = shard((z + k) % NZ, p)
        return remote(s, s, left_send.at[2 * k + p], left_recv.at[2 * k + p], down_z)

    for p in range(2):
        go_right(0, p).start()
        go_left(0, p).start()
    for copy in local[1:4]:
        copy.wait()
    for copy in to_partner[2:5]:
        copy.wait_recv()

    def back(yy, to):
        return remote(
            obuf.at[yy, to], rsum.at[yy, b], rs_send.at[yy * NDP + to],
            rs_recv.at[yy * NDP + b], (to, ex),
        )

    def expert_block(yy):
        for h in range(2):
            first_half = active if h == 1 else (active | (yy == y))

            @pl.when(jnp.logical_not((yy == y) & first_half))
            def _():
                wait_spread(yy, h)

        x = xbuf[yy]
        hidden = [
            (silu(dot_nt(x, wg[h])) * dot_nt(x, wu[h])).astype(BF16) for h in range(2)
        ]
        for n in range(NDP // 2):
            cols = pl.ds(n * 2 * COLS, 2 * COLS)
            value = (dot(hidden[0], wd[0, :, cols]) + dot(hidden[1], wd[1, :, cols])).astype(BF16)
            obuf[yy, 2 * n] = value[:, 0:COLS]
            obuf[yy, 2 * n + 1] = value[:, COLS:2 * COLS]

        @pl.loop(1, NDP)
        def _(k):
            back(yy, (b + k) % NDP).start()

    @pl.loop(1, 8)
    def _(k):
        for p in range(2):
            go_right(k - 1, p).wait_recv()
            go_right(k, p).start()
            go_left(k - 1, p).wait_recv()

            @pl.when(k < 7)
            def _():
                go_left(k, p).start()

        @pl.when((k >= 3) & (k < 7))
        def _():
            expert_block(k - 3)

    for p in range(2):
        go_right(7, p).wait_recv()

    local[4].wait()
    to_partner[1].wait_recv()
    relay.wait_recv()
    both = dot(tq[...], dense_w[:, 0:384])
    gu[...] = both[0:2 * NT]
    gu_send[...] = both[2 * NT:4 * NT].astype(BF16)
    gu_across = remote(gu_send, gu_recv, ac_send.at[1], ac_recv.at[1], across)
    gu_across.start()

    widen_col = iota((8 * SLOT, BLOCK), 1)
    widen = ones_where(
        iota((8 * SLOT, BLOCK), 0) == (widen_col // CAP) * SLOT + widen_col % CAP
    )

    def give(yy, s):
        s_x, s_z, s_c = source_of(2 * yy + core, s)
        return remote(
            slab(tbuf.at[yy], s), slab(ret, chip), ret_send.at[yy * 8 + s],
            ret_recv.at[chip], dev(b, s_x, s_z, s_c),
        )

    def sum_block(yy):
        @pl.loop(1, NDP)
        def _(k):
            src = (b + k) % NDP
            remote(
                obuf.at[yy, 0], rsum.at[yy, src], rs_send.at[0],
                rs_recv.at[yy * NDP + src], partner,
            ).wait_recv()

        total = obuf[yy, b].astype(F32)
        for k in range(1, NDP):
            total = total + rsum[yy, (b + k) % NDP].astype(F32)
        tbuf[yy] = dot(widen, total.astype(BF16)).astype(BF16)

        @pl.loop(0, 8)
        def _(s):
            give(yy, s).start()

    sum_block(0)

    gu_across.wait_recv()
    both = gu[...] + gu_recv[...].astype(F32)
    dense_hidden = silu(both) * pltpu.roll(both, 384 - HH, 1)
    dense_hidden = jnp.where(iota((2 * NT, 384), 1) < HH, dense_hidden, 0.0)
    hbuf[0:2 * NT] = pltpu.roll(dense_hidden, 2 * HH - 256, 1)[:, 0:256].astype(BF16)
    h_across = remote(
        hbuf.at[pl.ds(0, 2 * NT)], hbuf.at[pl.ds(2 * NT, 2 * NT)], ac_send.at[2], ac_recv.at[2],
        across,
    )
    h_across.start()

    sum_block(1)
    sum_block(2)

    h_across.wait_recv()
    for n in range(HALF // PIECE):
        cols = pl.ds(n * PIECE, PIECE)
        part = dot_nt(hbuf[...], dense_w[n * PIECE:(n + 1) * PIECE, 256:512])
        for t in range(2):
            d_mine[t, :, cols] = part[2 * t * NT:(2 * t + 1) * NT]
            d_send[t, :, cols] = part[(2 * t + 1) * NT:(2 * t + 2) * NT].astype(BF16)
    swap = remote(d_send, d_recv, core_send.at[6], core_recv.at[6], partner)
    swap.start()

    sum_block(3)

    swap.wait_recv()

    def finish(t, q):
        to = 4 * xl + q
        to_x = (xl + t) % 2
        return remote(
            dterm.at[t, q], fin.at[b], fin_send.at[t * 4 + q], fin_recv.at[b],
            dev(to, to_x, z, core),
        )

    for t in range(2):
        for n in range(2):
            cols = pl.ds(n * 2 * COLS, 2 * COLS)
            value = (d_mine[t, :, cols] + d_recv[t, :, cols].astype(F32)).astype(BF16)
            dterm[t, 2 * n] = value[:, 0:COLS]
            dterm[t, 2 * n + 1] = value[:, COLS:2 * COLS]

    def others(t, q):
        return jnp.logical_not(own_half & (t == 0) & (4 * xl + q == b))

    @pl.loop(0, 8)
    def _(n):
        @pl.when(others(n // 4, n % 4))
        def _():
            finish(n // 4, n % 4).start()

    @pl.when(own_half)
    def _():
        fin[b] = dterm[0, b % 4]

    @pl.loop(0, EXPERTS)
    def _(e):
        remote(
            slab(tbuf.at[0], 0), slab(ret, e), ret_send.at[0], ret_recv.at[e], partner
        ).wait_recv()

    rows = ret[...]
    total = dot(share_hi, rows) + dot(share_lo, rows)

    @pl.loop(0, NDP)
    def _(k):
        @pl.when(jnp.logical_not(own_half & (k == b)))
        def _():
            remote(
                dterm.at[0, 0], fin.at[k], fin_send.at[0], fin_recv.at[k], partner
            ).wait_recv()

    for k in range(NDP):
        total = total + fin[k].astype(F32)
    out[...] = total.astype(BF16)

    for copy in to_partner:
        copy.wait_send()
    for copy in (tok_across, relay, gu_across, h_across, swap):
        copy.wait_send()

    @pl.loop(0, 8)
    def _(n):
        dispatch(n // 4, n % 4).wait_send()

        for p in range(2):
            go_right(n, p).wait_send()

            @pl.when(n < 7)
            def _():
                go_left(n, p).wait_send()

        @pl.when(others(n // 4, n % 4))
        def _():
            finish(n // 4, n % 4).wait_send()

    @pl.loop(0, EXPERTS)
    def _(n):
        give(n // 8, n % 8).wait_send()

        @pl.when(n % 8 != b)
        def _():
            back(n // 8, n % 8).wait_send()

    @pl.when(active)
    def _():
        @pl.loop(1, NDP)
        def _(k):
            spread(0, k).wait_send()
            spread(1, k).wait_send()


def per_device(
    tokens, routes, gate_weights, w_dense_gate, w_dense_up, w_dense_down,
    w_exp_gate, w_exp_up, w_exp_down,
):
    rows = w_dense_gate.shape[0]
    vmem = pl.BlockSpec(memory_space=pltpu.VMEM)
    hbm = pl.BlockSpec(memory_space=pl.ANY)
    dma = pltpu.SemaphoreType.DMA
    return pl.pallas_call(
        kernel,
        out_shape=jax.ShapeDtypeStruct((NT, COLS), BF16),
        in_specs=[vmem] * 5 + [hbm] * 4,
        out_specs=vmem,
        scratch_shapes=[
            pltpu.VMEM((NT, D), BF16),
            pltpu.VMEM((4 * NT, HALF), BF16),
            pltpu.VMEM((4 * SLOT, D), BF16),
            pltpu.VMEM((8 * SLOT, D), BF16),
            pltpu.VMEM((NY, BLOCK, D), BF16),
            pltpu.VMEM((NY, NDP, BLOCK, COLS), BF16),
            pltpu.VMEM((NY, NDP, BLOCK, COLS), BF16),
            pltpu.VMEM((NY, 8 * SLOT, COLS), BF16),
            pltpu.VMEM((EXPERTS * SLOT, COLS), BF16),
            pltpu.VMEM((2, HH, D), BF16),
            pltpu.VMEM((2, HH, D), BF16),
            pltpu.VMEM((2, HH, D), BF16),
            pltpu.VMEM((2, rows, CHUNK), BF16),
            pltpu.VMEM((rows, CHUNK), BF16),
            pltpu.VMEM((HALF, CHUNK), BF16),
            pltpu.VMEM((2 * NT, 384), F32),
            pltpu.VMEM((2 * NT, 384), BF16),
            pltpu.VMEM((2 * NT, 384), BF16),
            pltpu.VMEM((4 * NT, 256), BF16),
            pltpu.VMEM((2, NT, HALF), F32),
            pltpu.VMEM((2, NT, HALF), BF16),
            pltpu.VMEM((2, NT, HALF), BF16),
            pltpu.VMEM((2, 4, NT, COLS), BF16),
            pltpu.VMEM((NDP, NT, COLS), BF16),
            dma((5,)), dma((7,)), dma((7,)), dma((3,)), dma((3,)), dma((8,)), dma((16,)),
            dma((14,)), dma((8,)), dma((16,)), dma((16,)), dma((14,)), dma((14,)),
            dma((32,)), dma((32,)), dma((32,)), dma((32,)), dma((8,)), dma((8,)),
        ],
        compiler_params=pltpu.CompilerParams(
            collective_id=0, has_side_effects=True, vmem_limit_bytes=56 * 1024 * 1024
        ),
    )(
        routes.T, gate_weights.T, w_dense_gate, w_dense_up, w_dense_down.T, tokens,
        w_exp_gate[0, 0].T, w_exp_up[0, 0].T, w_exp_down[0, 0],
    )


def solution(mesh):
    in_specs = (
        P("expert", None),
        P("expert", None),
        P("expert", None),
        P("expert", "dp"),
        P("expert", "dp"),
        P("dp", "expert"),
        P("dp", "expert", None, None),
        P("dp", "expert", None, None),
        P("dp", "expert", None, None),
    )
    return jax.shard_map(
        per_device, mesh=mesh, in_specs=in_specs, out_specs=P("expert", "dp"), check_vma=False
    )
```

time: 987 us -> 133 us (0.13)
  the two profiles are of different devices: /device:TPU:32 before, /device:TPU:61 now
where the time goes in v3:
time: 133 us
  Pallas kernels  131 us (98%)
  local copies, waits for them, and re-layouts  1.67 us (1%)
    pallas_call x1, Pallas kernels, per_device(): pl.pallas_call(kernel, out_shape=jax.ShapeDtypeStruct((NT, COLS), BF16),...  131 us

profile of v3, /device:TPU:61, one launch (start us, length us, event | category | flops | bytes accessed | tf_op | source)
XLA Modules:
  0.0 133.0 jit_solution(11598466457353120059)
XLA Ops:
  0.0 131.3 %shard_map.91 = bf16[128,448]{1,0:T(8,128)(2,1)} custom-call(s32[2,128]{1,0:T(2,128)} %bitcast.14, f32[2,128]{1,0:T(2,128)} %bitcast.15, bf16[56,304]{1,0:T(8,128)(2,1)} %dg.1, bf16[56,304]{1,0:T(8,128)(2,1)} %du.1, bf16[56,304]{1,0:T(8,128)(2,1)} %bitcast.13, bf16[128,3584]{1,0:T(8,128)(2,1)} %tok_hbm.1, bf16[152,3584]{1,0:T(8,128)(2,1)} %bitcast.10, ...), custom_call_target="tpu_custom_call" | custom-call | tf_op jit(solution)/shard_map/pallas_call | solution.py:492
  131.3 1.7 %copy.10 = bf16[128,448]{0,1:T(8,128)(2,1)} copy(bf16[128,448]{1,0:T(8,128)(2,1)} %shard_map.91) | data formatting | bytes 229376 | tf_op jit(solution)/shard_map/pallas_call | solution.py:492

commit v4 on v3

--- a/solution.py
+++ b/solution.py
@@ -55,11 +55,11 @@
 
 def kernel(
     routes_t, weights_t, dg, du, dd_t, tok_hbm, wg_hbm, wu_hbm, wd_hbm, out,
-    tok, tq, sbuf, rbuf, xbuf, obuf, rsum, tbuf, ret, wg, wu, wd, pack, theirs, dense_w,
-    gu, gu_send, gu_recv, hbuf, d_mine, d_send, d_recv, dterm, fin,
-    loc, core_send, core_recv, ac_send, ac_recv, dis_send, dis_recv, bc_send, bc_recv,
+    tok, tq, sbuf, rbuf, xbuf, obuf, rsum, keep, cross, crossed, tbuf, ret, wg, wu, wd, pack, theirs, dense_w,
+    acc, hidv, gu, gu_send, gu_recv, hbuf, d_mine, d_send, d_recv, dterm, fin,
+    loc, core_send, core_recv, ac_send, ac_recv, dis_send, dis_recv, bx_send, by_send, bp_send, bc_recv,
     right_send, right_recv, left_send, left_recv,
-    rs_send, rs_recv, ret_send, ret_recv, fin_send, fin_recv,
+    rs_send, rs_recv, cx_send, cx_recv, ret_send, ret_recv, fin_send, fin_recv,
 ):
     b = lax.axis_index("dp")
     ex = lax.axis_index("expert")
@@ -68,7 +68,8 @@
     z = chip % NZ
     xl = chip // NZ
     y = b // 2
-    active = (b % 2) == core
+    side = b % 2
+    active = side == core
     own_half = (b // 4) == xl
 
     def dev(bb, xx, zz, cc):
@@ -114,11 +115,13 @@
     up_z = dev(b, xl, (z + 1) % NZ, core)
     down_z = dev(b, xl, (z + NZ - 1) % NZ, core)
 
-    @pl.loop(1, NDP)
-    def _(k):
-        greet(((b + k) % NDP, ex))
-
-    for to in (partner, across, up_z, down_z):
+    def along_y(d):
+        return (((y + d) % NY) * 2 + side, ex)
+
+    across_hi = (2 * y + 1 - side, ex)
+    for to in (
+        along_y(1), along_y(2), along_y(3), across_hi, partner, across, up_z, down_z
+    ):
         greet(to)
 
     @pl.when(active)
@@ -164,7 +167,7 @@
         pack[h] = total.astype(BF16)
 
     pl.semaphore_wait(
-        barrier, jnp.where(own_half, 7, 8) + 7 + 4 + 4 + EXPERTS
+        barrier, jnp.where(own_half, 7, 8) + 8 + 4 + EXPERTS
     )
 
     def dispatch(h, k):
@@ -216,19 +219,53 @@
         iota((BLOCK, 8 * SLOT), 1) == (slot_row // CAP) * SLOT + slot_row % CAP
     )
 
+    def block_rows(yy):
+        return pl.ds(pl.multiple_of(yy * BLOCK, 16), BLOCK)
+
     def x_part(yy, h):
-        return xbuf.at[yy, :, pl.ds(pl.multiple_of(h * HALF, 128), HALF)]
-
-    def spread(h, k):
-        return remote(
-            x_part(y, h), x_part(y, h), bc_send.at[h * 7 + k - 1], bc_recv.at[h * 4 + y],
-            ((b + k) % NDP, ex),
-        )
+        return xbuf.at[block_rows(yy), pl.ds(pl.multiple_of(h * HALF, 128), HALF)]
 
     def wait_spread(yy, h):
         remote(
-            x_part(yy, h), x_part(yy, h), bc_send.at[0], bc_recv.at[h * 4 + yy], partner
+            x_part(yy, h), x_part(yy, h), bx_send.at[0], bc_recv.at[h * NY + yy], partner
         ).wait_recv()
+
+    def spread_x(h):
+        return remote(
+            x_part(y, h), x_part(y, h), bx_send.at[h], bc_recv.at[h * NY + y], across_hi
+        )
+
+    def spread_y(h, n):
+        return remote(
+            x_part(y, h), x_part(y, h), by_send.at[2 * h + n], bc_recv.at[h * NY + y],
+            along_y(1 + 2 * n),
+        )
+
+    def pass_on(h):
+        yy = (y + 3 - 2 * h) % NY
+        return remote(
+            x_part(yy, h), x_part(yy, h), bp_send.at[h], bc_recv.at[h * NY + yy],
+            along_y(1 + 2 * h),
+        )
+
+    def shard(zz, p):
+        return dense_w.at[
+            pl.ds(pl.multiple_of(zz * CHIP_ROWS, 16), CHIP_ROWS),
+            pl.ds(p * PIECE, PIECE),
+        ]
+
+    def go_right(k, p):
+        s = shard((z + NZ - k) % NZ, p)
+        return remote(s, s, right_send.at[2 * k + p], right_recv.at[2 * k + p], up_z)
+
+    def go_left(k, p):
+        s = shard((z + k) % NZ, p)
+        return remote(s, s, left_send.at[2 * k + p], left_recv.at[2 * k + p], down_z)
+
+    def ring_start():
+        for p in range(2):
+            go_right(0, p).start()
+            go_left(0, p).start()
 
     @pl.when(active)
     def _():
@@ -242,11 +279,14 @@
                     dis_send.at[0], dis_recv.at[h * 8 + s], partner,
                 ).wait_recv()
 
-            xbuf[y, :, cols] = dot(squeeze, rbuf[:, cols]).astype(BF16)
-
-            @pl.loop(1, NDP)
-            def _(k):
-                spread(h, k).start()
+            xbuf[block_rows(y), cols] = dot(squeeze, rbuf[:, cols]).astype(BF16)
+
+            spread_x(h).start()
+            for n in range(2):
+                spread_y(h, n).start()
+
+            if h == 0:
+                ring_start()
 
     tok_across.wait_recv()
     relay = remote(
@@ -258,56 +298,90 @@
     @pl.when(jnp.logical_not(active))
     def _():
         wait_spread(y, 0)
-
-    def shard(zz, p):
-        return dense_w.at[
-            pl.ds(pl.multiple_of(zz * CHIP_ROWS, 16), CHIP_ROWS),
-            pl.ds(p * PIECE, PIECE),
-        ]
-
-    def go_right(k, p):
-        s = shard((z + NZ - k) % NZ, p)
-        return remote(s, s, right_send.at[2 * k + p], right_recv.at[2 * k + p], up_z)
-
-    def go_left(k, p):
-        s = shard((z + k) % NZ, p)
-        return remote(s, s, left_send.at[2 * k + p], left_recv.at[2 * k + p], down_z)
-
-    for p in range(2):
-        go_right(0, p).start()
-        go_left(0, p).start()
+        for n in range(2):
+            spread_y(0, n).start()
+        ring_start()
+
     for copy in local[1:4]:
         copy.wait()
     for copy in to_partner[2:5]:
         copy.wait_recv()
 
-    def back(yy, to):
-        return remote(
-            obuf.at[yy, to], rsum.at[yy, b], rs_send.at[yy * NDP + to],
-            rs_recv.at[yy * NDP + b], (to, ex),
-        )
+    def back(yy, d):
+        to = (y + d) % NY
+        return remote(
+            obuf.at[yy, to], rsum.at[yy, y], rs_send.at[yy * NY + d], rs_recv.at[yy * NY + y],
+            along_y(d),
+        )
+
+    def gate_up(h):
+        cols = pl.ds(h * HALF, HALF)
+        x = xbuf[:, cols]
+        return [dot_nt(x, w[half, :, cols]) for half in range(2) for w in (wg, wu)]
+
+    def experts_first():
+        wait_spread((y + 1) % NY, 0)
+        wait_spread((y + 2) % NY, 0)
+        for n, part in enumerate(gate_up(0)):
+            acc[n] = part
+
+    def experts_second():
+        wait_spread((y + 3) % NY, 1)
+        wait_spread((y + 2) % NY, 1)
+        parts = [acc[n] + part for n, part in enumerate(gate_up(1))]
+        for half in range(2):
+            hidv[half] = (silu(parts[2 * half]) * parts[2 * half + 1]).astype(BF16)
 
     def expert_block(yy):
-        for h in range(2):
-            first_half = active if h == 1 else (active | (yy == y))
-
-            @pl.when(jnp.logical_not((yy == y) & first_half))
-            def _():
-                wait_spread(yy, h)
-
-        x = xbuf[yy]
-        hidden = [
-            (silu(dot_nt(x, wg[h])) * dot_nt(x, wu[h])).astype(BF16) for h in range(2)
-        ]
-        for n in range(NDP // 2):
+        hidden = [hidv[half, yy * BLOCK:(yy + 1) * BLOCK] for half in range(2)]
+        for n in range(NY):
             cols = pl.ds(n * 2 * COLS, 2 * COLS)
-            value = (dot(hidden[0], wd[0, :, cols]) + dot(hidden[1], wd[1, :, cols])).astype(BF16)
-            obuf[yy, 2 * n] = value[:, 0:COLS]
-            obuf[yy, 2 * n + 1] = value[:, COLS:2 * COLS]
-
-        @pl.loop(1, NDP)
-        def _(k):
-            back(yy, (b + k) % NDP).start()
+            obuf[yy, n] = (
+                dot(hidden[0], wd[0, :, cols]) + dot(hidden[1], wd[1, :, cols])
+            ).astype(BF16)
+
+        for d in range(1, NY):
+            back(yy, d).start()
+
+    widen_col = iota((8 * SLOT, BLOCK), 1)
+    widen = ones_where(
+        iota((8 * SLOT, BLOCK), 0) == (widen_col // CAP) * SLOT + widen_col % CAP
+    )
+
+    def give(yy, s):
+        s_x, s_z, s_c = source_of(2 * yy + core, s)
+        return remote(
+            slab(tbuf.at[yy], s), slab(ret, chip), ret_send.at[yy * 8 + s],
+            ret_recv.at[chip], dev(b, s_x, s_z, s_c),
+        )
+
+    def sum_y(yy):
+        total = obuf[yy, y].astype(F32)
+        for d in range(1, NY):
+            src = (y + d) % NY
+            remote(
+                obuf.at[yy, 0], rsum.at[yy, src], rs_send.at[0],
+                rs_recv.at[yy * NY + src], partner,
+            ).wait_recv()
+            total = total + rsum[yy, src].astype(F32)
+        low, high = total[:, 0:COLS], total[:, COLS:2 * COLS]
+        keep[yy] = jnp.where(side == 0, low, high)
+        cross[yy] = jnp.where(side == 0, high, low).astype(BF16)
+        cross_x(yy).start()
+
+    def cross_x(yy):
+        return remote(
+            cross.at[yy], crossed.at[yy], cx_send.at[yy], cx_recv.at[yy], across_hi
+        )
+
+    def sum_x(yy):
+        cross_x(yy).wait_recv()
+        total = keep[yy] + crossed[yy].astype(F32)
+        tbuf[yy] = dot(widen, total.astype(BF16)).astype(BF16)
+
+        @pl.loop(0, 8)
+        def _(s):
+            give(yy, s).start()
 
     @pl.loop(1, 8)
     def _(k):
@@ -320,9 +394,32 @@
             def _():
                 go_left(k, p).start()
 
-        @pl.when((k >= 3) & (k < 7))
-        def _():
-            expert_block(k - 3)
+        @pl.when(k == 1)
+        def _():
+            wait_spread((y + 3) % NY, 0)
+            pass_on(0).start()
+
+            @pl.when(jnp.logical_not(active))
+            def _():
+                wait_spread(y, 1)
+                for n in range(2):
+                    spread_y(1, n).start()
+
+        @pl.when(k == 3)
+        def _():
+            wait_spread((y + 1) % NY, 1)
+            pass_on(1).start()
+            experts_first()
+
+        @pl.when(k == 5)
+        def _():
+            experts_second()
+            for yy in range(NY):
+                expert_block(yy)
+
+        @pl.when(k == 7)
+        def _():
+            sum_y(0)
 
     for p in range(2):
         go_right(7, p).wait_recv()
@@ -336,37 +433,8 @@
     gu_across = remote(gu_send, gu_recv, ac_send.at[1], ac_recv.at[1], across)
     gu_across.start()
 
-    widen_col = iota((8 * SLOT, BLOCK), 1)
-    widen = ones_where(
-        iota((8 * SLOT, BLOCK), 0) == (widen_col // CAP) * SLOT + widen_col % CAP
-    )
-
-    def give(yy, s):
-        s_x, s_z, s_c = source_of(2 * yy + core, s)
-        return remote(
-            slab(tbuf.at[yy], s), slab(ret, chip), ret_send.at[yy * 8 + s],
-            ret_recv.at[chip], dev(b, s_x, s_z, s_c),
-        )
-
-    def sum_block(yy):
-        @pl.loop(1, NDP)
-        def _(k):
-            src = (b + k) % NDP
-            remote(
-                obuf.at[yy, 0], rsum.at[yy, src], rs_send.at[0],
-                rs_recv.at[yy * NDP + src], partner,
-            ).wait_recv()
-
-        total = obuf[yy, b].astype(F32)
-        for k in range(1, NDP):
-            total = total + rsum[yy, (b + k) % NDP].astype(F32)
-        tbuf[yy] = dot(widen, total.astype(BF16)).astype(BF16)
-
-        @pl.loop(0, 8)
-        def _(s):
-            give(yy, s).start()
-
-    sum_block(0)
+    sum_x(0)
+    sum_y(1)
 
     gu_across.wait_recv()
     both = gu[...] + gu_recv[...].astype(F32)
@@ -379,8 +447,8 @@
     )
     h_across.start()
 
-    sum_block(1)
-    sum_block(2)
+    sum_y(2)
+    sum_x(1)
 
     h_across.wait_recv()
     for n in range(HALF // PIECE):
@@ -392,7 +460,8 @@
     swap = remote(d_send, d_recv, core_send.at[6], core_recv.at[6], partner)
     swap.start()
 
-    sum_block(3)
+    sum_y(3)
+    sum_x(2)
 
     swap.wait_recv()
 
@@ -424,6 +493,8 @@
     def _():
         fin[b] = dterm[0, b % 4]
 
+    sum_x(3)
+
     @pl.loop(0, EXPERTS)
     def _(e):
         remote(
@@ -469,16 +540,21 @@
     def _(n):
         give(n // 8, n % 8).wait_send()
 
-        @pl.when(n % 8 != b)
-        def _():
-            back(n // 8, n % 8).wait_send()
+    @pl.loop(0, NY)
+    def _(yy):
+        cross_x(yy).wait_send()
+        for d in range(1, NY):
+            back(yy, d).wait_send()
+
+    for h in range(2):
+        pass_on(h).wait_send()
+        for n in range(2):
+            spread_y(h, n).wait_send()
 
     @pl.when(active)
     def _():
-        @pl.loop(1, NDP)
-        def _(k):
-            spread(0, k).wait_send()
-            spread(1, k).wait_send()
+        for h in range(2):
+            spread_x(h).wait_send()
 
 
 def per_device(
@@ -499,9 +575,12 @@
             pltpu.VMEM((4 * NT, HALF), BF16),
             pltpu.VMEM((4 * SLOT, D), BF16),
             pltpu.VMEM((8 * SLOT, D), BF16),
-            pltpu.VMEM((NY, BLOCK, D), BF16),
-            pltpu.VMEM((NY, NDP, BLOCK, COLS), BF16),
-            pltpu.VMEM((NY, NDP, BLOCK, COLS), BF16),
+            pltpu.VMEM((NY * BLOCK, D), BF16),
+            pltpu.VMEM((NY, NY, BLOCK, 2 * COLS), BF16),
+            pltpu.VMEM((NY, NY, BLOCK, 2 * COLS), BF16),
+            pltpu.VMEM((NY, BLOCK, COLS), F32),
+            pltpu.VMEM((NY, BLOCK, COLS), BF16),
+            pltpu.VMEM((NY, BLOCK, COLS), BF16),
             pltpu.VMEM((NY, 8 * SLOT, COLS), BF16),
             pltpu.VMEM((EXPERTS * SLOT, COLS), BF16),
             pltpu.VMEM((2, HH, D), BF16),
@@ -510,6 +589,8 @@
             pltpu.VMEM((2, rows, CHUNK), BF16),
             pltpu.VMEM((rows, CHUNK), BF16),
             pltpu.VMEM((HALF, CHUNK), BF16),
+            pltpu.VMEM((4, NY * BLOCK, HH), F32),
+            pltpu.VMEM((2, NY * BLOCK, HH), BF16),
             pltpu.VMEM((2 * NT, 384), F32),
             pltpu.VMEM((2 * NT, 384), BF16),
             pltpu.VMEM((2 * NT, 384), BF16),
@@ -520,8 +601,10 @@
             pltpu.VMEM((2, 4, NT, COLS), BF16),
             pltpu.VMEM((NDP, NT, COLS), BF16),
             dma((5,)), dma((7,)), dma((7,)), dma((3,)), dma((3,)), dma((8,)), dma((16,)),
-            dma((14,)), dma((8,)), dma((16,)), dma((16,)), dma((14,)), dma((14,)),
-            dma((32,)), dma((32,)), dma((32,)), dma((32,)), dma((8,)), dma((8,)),
+            dma((2,)), dma((4,)), dma((2,)), dma((8,)),
+            dma((16,)), dma((16,)), dma((14,)), dma((14,)),
+            dma((16,)), dma((16,)), dma((4,)), dma((4,)), dma((32,)), dma((32,)),
+            dma((8,)), dma((8,)),
         ],
         compiler_params=pltpu.CompilerParams(
             collective_id=0, has_side_effects=True, vmem_limit_bytes=56 * 1024 * 1024

time: 133 us -> 120 us (0.902)
  the two profiles are of different devices: /device:TPU:61 before, /device:TPU:43 now
where the time goes in v4:
time: 120 us; the launch traced here: 118 us
  Pallas kernels  117 us (98%)
  local copies, waits for them, and re-layouts  1.67 us (1%)
    pallas_call x1, Pallas kernels, per_device(): pl.pallas_call(kernel, out_shape=jax.ShapeDtypeStruct((NT, COLS), BF16),...  117 us

profile of v4, /device:TPU:43, one launch (start us, length us, event | category | flops | bytes accessed | tf_op | source)
XLA Modules:
  0.0 118.4 jit_solution(17193203913872128135)
XLA Ops:
  0.0 116.7 %shard_map.91 = bf16[128,448]{1,0:T(8,128)(2,1)} custom-call(s32[2,128]{1,0:T(2,128)} %bitcast.14, f32[2,128]{1,0:T(2,128)} %bitcast.15, bf16[56,304]{1,0:T(8,128)(2,1)} %dg.1, bf16[56,304]{1,0:T(8,128)(2,1)} %du.1, bf16[56,304]{1,0:T(8,128)(2,1)} %bitcast.13, bf16[128,3584]{1,0:T(8,128)(2,1)} %tok_hbm.1, bf16[152,3584]{1,0:T(8,128)(2,1)} %bitcast.10, ...), custom_call_target="tpu_custom_call" | custom-call | tf_op jit(solution)/shard_map/pallas_call | solution.py:568
  116.7 1.7 %copy.10 = bf16[128,448]{0,1:T(8,128)(2,1)} copy(bf16[128,448]{1,0:T(8,128)(2,1)} %shard_map.91) | data formatting | bytes 229376 | tf_op jit(solution)/shard_map/pallas_call | solution.py:568

commit v5 on v4

v5 whole, which is shorter than its diff:
```python
import jax
import jax.numpy as jnp
from jax import lax
from jax.experimental import pallas as pl
from jax.experimental.pallas import tpu as pltpu
from jax.sharding import PartitionSpec as P

CAP = 10
TILE = 128
TILES = 14
SEND = 144
BACK = 48
NZ = 16
NY = 4
NDP = 8
NT = 128
D = 3584
HALF = D // 2
HH = 152
BLOCK = 8 * CAP
CHIP_ROWS = 112
COLS = 448
CHUNK = 512
PIECE = 256
EXPERTS = 32
MESH = pl.DeviceIdType.MESH
F32 = jnp.float32
BF16 = jnp.bfloat16


def dz_of(j, xl_to, i):
    d = jnp.where(xl_to == 0, j, 8 - j)
    edge = (d % 8) == 0
    first = jnp.where(edge, 0, d)
    second = jnp.where(edge, 8, NZ - d)
    return jnp.where(i == 0, first, second)


def iota(shape, dim):
    return lax.broadcasted_iota(jnp.int32, shape, dim)


def ones_where(mask):
    return jnp.where(mask, 1.0, 0.0).astype(BF16)


def dot(a, b):
    return jnp.dot(a, b, preferred_element_type=F32)


def dot_nt(a, b):
    return lax.dot_general(a, b, (((1,), (1,)), ((), ())), preferred_element_type=F32)


def silu(v):
    return v / (1.0 + jnp.exp(-v))


def kernel(
    routes_t, weights_t, dg, du, dd_t, tok_hbm, wg_hbm, wu_hbm, wd_hbm, out,
    tok, tq, sbuf, rbuf, squeeze, shares, xbuf, hcat, keep, cross, crossed, tbuf, ret, wg, wu, wall, pack, theirs, dense_w,
    acc, gu, gu_send, gu_recv, hbuf, d_mine, d_send, d_recv, dterm, fin,
    loc, core_send, core_recv, ac_send, ac_recv, dis_send, dis_recv, bx_send, by_send, bp_send, bc_recv,
    right_send, right_recv, left_send, left_recv,
    wa_send, wa_recv, cx_send, cx_recv, hy_send, hp_send, hy_recv, ret_send, ret_recv, fin_send, fin_recv,
):
    b = lax.axis_index("dp")
    ex = lax.axis_index("expert")
    core = ex % 2
    chip = ex // 2
    z = chip % NZ
    xl = chip // NZ
    y = b // 2
    side = b % 2
    active = side == core
    own_half = (b // 4) == xl

    def dev(bb, xx, zz, cc):
        return (bb, (xx * NZ + zz) * 2 + cc)

    def remote(src, dst, send, recv, to):
        return pltpu.make_async_remote_copy(
            src_ref=src, dst_ref=dst, send_sem=send, recv_sem=recv, device_id=to,
            device_id_type=MESH,
        )

    def dest_of(bb, k):
        to_x, i = k // 2, k % 2
        return to_x, (z + dz_of((bb + 15 - core) % 8, to_x, i)) % NZ

    def source_of(bb, slot):
        i, s_x, s_c = slot // 4, (slot // 2) % 2, slot % 2
        return s_x, (z + NZ - dz_of((bb + 15 - s_c) % 8, xl, i)) % NZ, s_c

    def rows_of(n, size):
        return pl.ds(pl.multiple_of(n * size, 16), size)

    def pair_of(yy):
        return wd_hbm.at[:, pl.ds(pl.multiple_of(yy * 2 * COLS, 128), 2 * COLS)]

    def tok_half(which):
        return tok_hbm.at[:, pl.ds(pl.multiple_of(which * HALF, 128), HALF)]

    local = [
        pltpu.make_async_copy(tok_hbm, tok, loc.at[0]),
        pltpu.make_async_copy(wg_hbm, wg.at[0], loc.at[1]),
        pltpu.make_async_copy(wu_hbm, wu.at[0], loc.at[2]),
        pltpu.make_async_copy(pair_of(y), wall.at[0, y], loc.at[3]),
        pltpu.make_async_copy(tok_half(xl), tq.at[pl.ds(0, NT)], loc.at[4]),
    ]
    for copy in local:
        copy.start()

    barrier = pltpu.get_barrier_semaphore()

    def greet(to):
        pl.semaphore_signal(barrier, inc=1, device_id=to, device_id_type=MESH)

    partner = (b, chip * 2 + 1 - core)
    across = dev(b, 1 - xl, z, core)
    up_z = dev(b, xl, (z + 1) % NZ, core)
    down_z = dev(b, xl, (z + NZ - 1) % NZ, core)

    def along_y(d):
        return (((y + d) % NY) * 2 + side, ex)

    across_hi = (2 * y + 1 - side, ex)
    for to in (partner, across, up_z, down_z):
        greet(to)

    for to in (along_y(1), along_y(2), along_y(3), across_hi):
        greet(to)

    @pl.when(active)
    def _():
        @pl.loop(0, 8)
        def _(s):
            s_x, s_z, s_c = source_of(b, s)
            greet(dev(b, s_x, s_z, s_c))

    @pl.loop(0, EXPERTS)
    def _(n):
        bb = n // 4
        to_x, to_z = dest_of(bb, n % 4)
        greet(dev(b, to_x, to_z, bb % 2))

    @pl.loop(0, NDP)
    def _(k):
        @pl.when(jnp.logical_not(own_half & (k == b)))
        def _():
            greet(dev(k, b // 4, z, core))

    row = iota((4 * SEND, NT), 0)
    k_row, at = row // SEND, row % SEND
    e_row = (k_row // 2) * NZ + (z + dz_of((b + 15 - core) % 8, k_row // 2, k_row % 2)) % NZ
    hit = (routes_t[0:1, :] == e_row) | (routes_t[1:2, :] == e_row)
    before = ones_where(iota((NT, NT), 0) < iota((NT, NT), 1))
    rank = dot(ones_where(hit), before)
    select = jnp.where(hit & (rank == (at % CAP).astype(F32)), 1.0, 0.0)
    tile_of = at // CAP

    groups = []
    for first, tiles, size in ((0, 8, 80), (8, 6, 64)):
        rows = [slice(k * SEND + first * CAP, k * SEND + first * CAP + size) for k in range(4)]
        groups.append((
            first, tiles, size,
            jnp.concatenate([select[r] for r in rows], axis=0),
            jnp.concatenate([tile_of[r] for r in rows], axis=0),
        ))

    def fill(h):
        for first, tiles, size, chosen, tile_at in groups:
            total = None
            for n in range(first, first + tiles):
                left = jnp.where(tile_at == n, chosen, 0.0).astype(BF16)
                part = dot(left, tok[:, h * HALF + n * TILE:h * HALF + (n + 1) * TILE])
                total = part if total is None else total + part
            total = total.astype(BF16)
            for k in range(4):
                start = k * SEND + first * CAP
                sbuf[h, start:start + size] = total[k * size:(k + 1) * size]

    local[0].wait()
    fill(0)

    hid = iota((2 * HH, CHUNK), 0)
    lane = iota((2 * HH, CHUNK), 1)
    for h in range(2):
        here = (hid >= h * HH) & (hid < (h + 1) * HH)
        total = None
        for n, part in enumerate((dg[...], du[...], dd_t[...])):
            placed = ones_where(here & (lane == hid - h * HH + n * HH))
            term = dot(part, placed)
            total = term if total is None else total + term
        pack[h] = total.astype(BF16)

    pl.semaphore_wait(
        barrier, jnp.where(own_half, 7, 8) + 8 + 4 + EXPERTS
    )

    def dispatch(h, k):
        to_x, to_z = dest_of(b, k)
        slot = (k % 2) * 4 + xl * 2 + core
        return remote(
            sbuf.at[h, rows_of(k, SEND)], rbuf.at[h, rows_of(slot, SEND)],
            dis_send.at[h * 4 + k], dis_recv.at[h * 8 + slot], dev(b, to_x, to_z, b % 2),
        )

    @pl.loop(0, 4)
    def _(n):
        dispatch(0, n).start()

    fill(1)

    @pl.loop(0, 4)
    def _(n):
        dispatch(1, n).start()

    def cut_to(d):
        return remote(
            pair_of((y + d) % NY), wall.at[0, y], wa_send.at[d - 1], wa_recv.at[y], along_y(d)
        )

    for d in range(1, NY):
        cut_to(d).start()

    to_partner = [
        remote(pack.at[1 - core], theirs, core_send.at[0], core_recv.at[0], partner),
        remote(tok_half(xl), tq.at[pl.ds(NT, NT)], core_send.at[1], core_recv.at[1], partner),
        remote(wg_hbm, wg.at[1], core_send.at[2], core_recv.at[2], partner),
        remote(wu_hbm, wu.at[1], core_send.at[3], core_recv.at[3], partner),
    ]
    for copy in to_partner:
        copy.start()
    tok_across = remote(
        tok_half(1 - xl), tq.at[pl.ds(2 * NT, NT)], ac_send.at[0], ac_recv.at[0], across
    )
    tok_across.start()

    place = iota((EXPERTS * BACK, NT), 0)
    hit0 = routes_t[0:1, :] == place // BACK
    hit1 = routes_t[1:2, :] == place // BACK
    rank_all = dot(ones_where(hit0 | hit1), before)
    share = jnp.where(hit0, weights_t[0:1, :], 0.0) + jnp.where(hit1, weights_t[1:2, :], 0.0)
    share = jnp.where(rank_all == ((place % BACK) % CAP).astype(F32), share, 0.0).T
    back_tile = (iota((NT, EXPERTS * BACK), 1) % BACK) // CAP
    for n in range(4):
        mine = jnp.where(back_tile == n, share, 0.0)
        mine_hi = mine.astype(BF16)
        shares[0, n * NT:(n + 1) * NT] = mine_hi
        shares[1, n * NT:(n + 1) * NT] = (mine - mine_hi.astype(F32)).astype(BF16)

    to_partner[0].wait_recv()
    mine = pack[core]
    first = jnp.where(core == 0, mine, theirs[...])
    second = jnp.where(core == 0, theirs[...], mine)
    dense_w[pl.ds(pl.multiple_of(z * CHIP_ROWS, 16), CHIP_ROWS), :] = jnp.concatenate(
        [first, second], axis=0
    )

    def block_rows(yy):
        return pl.ds(pl.multiple_of(yy * BLOCK, 16), BLOCK)

    def x_part(yy, h):
        return xbuf.at[block_rows(yy), pl.ds(pl.multiple_of(h * HALF, 128), HALF)]

    def wait_spread(yy, h):
        remote(
            x_part(yy, h), x_part(yy, h), bx_send.at[0], bc_recv.at[h * NY + yy], partner
        ).wait_recv()

    def spread_x(yy, h):
        return remote(
            x_part(yy, h), x_part(yy, h), bx_send.at[h * NY + yy], bc_recv.at[h * NY + yy],
            across_hi,
        )

    def spread_y(h, n):
        return remote(
            x_part(y, h), x_part(y, h), by_send.at[2 * h + n], bc_recv.at[h * NY + y],
            along_y(1 + 2 * n),
        )

    def pass_on(h):
        yy = (y + 3 - 2 * h) % NY
        return remote(
            x_part(yy, h), x_part(yy, h), bp_send.at[h], bc_recv.at[h * NY + yy],
            along_y(1 + 2 * h),
        )

    def shard(zz, p):
        return dense_w.at[
            pl.ds(pl.multiple_of(zz * CHIP_ROWS, 16), CHIP_ROWS),
            pl.ds(p * PIECE, PIECE),
        ]

    def go_right(k, p):
        s = shard((z + NZ - k) % NZ, p)
        return remote(s, s, right_send.at[2 * k + p], right_recv.at[2 * k + p], up_z)

    def go_left(k, p):
        s = shard((z + k) % NZ, p)
        return remote(s, s, left_send.at[2 * k + p], left_recv.at[2 * k + p], down_z)

    def ring_step(k):
        for p in range(2):
            go_right(k - 1, p).wait_recv()
            go_right(k, p).start()
            go_left(k - 1, p).wait_recv()

            @pl.when(k < 7)
            def _():
                go_left(k, p).start()

    for p in range(2):
        go_right(0, p).start()
        go_left(0, p).start()

    @pl.when(active)
    def _():
        slot_row = iota((BLOCK, 8 * SEND), 0)
        offset = iota((BLOCK, 8 * SEND), 1) - (slot_row // CAP) * SEND - slot_row % CAP
        for n in range(TILES):
            squeeze[n * BLOCK:(n + 1) * BLOCK] = ones_where(offset == n * CAP)

        for h in range(2):

            @pl.loop(0, 8)
            def _(s):
                remote(
                    sbuf.at[h, rows_of(0, SEND)], rbuf.at[h, rows_of(s, SEND)],
                    dis_send.at[0], dis_recv.at[h * 8 + s], partner,
                ).wait_recv()

            rows = dot(squeeze[...], rbuf[h]).astype(BF16)
            for n in range(TILES):
                xbuf[block_rows(y), h * HALF + n * TILE:h * HALF + (n + 1) * TILE] = rows[
                    n * BLOCK:(n + 1) * BLOCK
                ]

            spread_x(y, h).start()
            for n in range(2):
                spread_y(h, n).start()

    relay = remote(
        tq.at[pl.ds(2 * NT, NT)], tq.at[pl.ds(3 * NT, NT)], core_send.at[5], core_recv.at[5],
        partner,
    )

    @pl.when(jnp.logical_not(active))
    def _():
        ring_step(1)
        wait_spread(y, 0)
        for n in range(2):
            spread_y(0, n).start()

    for copy in local[1:4]:
        copy.wait()
    for copy in to_partner[2:4]:
        copy.wait_recv()

    wall_partner = remote(
        wall.at[0], wall.at[1], core_send.at[4], core_recv.at[4], partner
    )

    def hid_y(g, n):
        return remote(
            hcat.at[y, g], hcat.at[y, g], hy_send.at[2 * g + n], hy_recv.at[g * NY + y],
            along_y(1 + 2 * n),
        )

    def hid_pass(g):
        yy = (y + 3 - 2 * g) % NY
        return remote(
            hcat.at[yy, g], hcat.at[yy, g], hp_send.at[g], hy_recv.at[g * NY + yy],
            along_y(1 + 2 * g),
        )

    def wait_hid(yy, g):
        remote(
            hcat.at[yy, g], hcat.at[yy, g], hp_send.at[0], hy_recv.at[g * NY + yy], partner
        ).wait_recv()

    def gate_up(h):
        cols = pl.ds(h * HALF, HALF)
        x = xbuf[:, cols]
        return [dot_nt(x, w[half, :, cols]) for half in range(2) for w in (wg, wu)]

    def experts_first():
        wait_spread((y + 1) % NY, 0)
        wait_spread((y + 2) % NY, 0)
        for n, part in enumerate(gate_up(0)):
            acc[n] = part

    def experts_second():
        @pl.when(jnp.logical_not(active))
        def _():
            for d in range(NY):
                wait_spread((y + d) % NY, 1)

        parts = [acc[n] + part for n, part in enumerate(gate_up(1))]
        hidden = jnp.concatenate(
            [
                (silu(parts[2 * half]) * parts[2 * half + 1]).astype(BF16)
                for half in range(2)
            ],
            axis=1,
        )
        for g in range(2):
            hcat[y, g] = hidden[g * 2 * BLOCK:(g + 1) * 2 * BLOCK]
            for n in range(2):
                hid_y(g, n).start()

    wide_row = iota((8 * BACK, BLOCK), 0)
    wide_at = wide_row % BACK
    wide_tile = jnp.where(
        (wide_row // BACK) * CAP + wide_at % CAP == iota((8 * BACK, BLOCK), 1),
        wide_at // CAP, -1,
    )
    widen = [ones_where(wide_tile == n) for n in range(4)]

    def give(yy, s):
        s_x, s_z, s_c = source_of(2 * yy + core, s)
        return remote(
            tbuf.at[yy, rows_of(s, BACK)], ret.at[rows_of(chip, BACK)], ret_send.at[yy * 8 + s],
            ret_recv.at[chip], dev(b, s_x, s_z, s_c),
        )

    def cross_x(g):
        return remote(cross.at[g], crossed.at[g], cx_send.at[g], cx_recv.at[g], across_hi)

    def outputs(g):
        wait_hid((y + 1 + 2 * g) % NY, g)
        wait_hid((y + 2) % NY, g)
        total = None
        for yy in range(NY):
            value = hcat[yy, g]
            for half in range(2):
                part = dot(value[:, half * HH:(half + 1) * HH], wall[half, yy])
                total = part if total is None else total + part
        low, high = total[:, 0:COLS], total[:, COLS:2 * COLS]
        keep[g] = jnp.where(side == 0, low, high)
        cross[g] = jnp.where(side == 0, high, low).astype(BF16)
        cross_x(g).start()

    def finish_outputs(g):
        cross_x(g).wait_recv()
        total = keep[g] + crossed[g].astype(F32)
        total = jnp.concatenate(
            [total.astype(BF16), jnp.zeros((2 * BLOCK, 4 * TILE - COLS), BF16)], axis=1
        )
        for i in range(2):
            wide = None
            for n in range(4):
                part = dot(
                    widen[n], total[i * BLOCK:(i + 1) * BLOCK, n * TILE:(n + 1) * TILE]
                )
                wide = part if wide is None else wide + part
            tbuf[2 * g + i] = wide.astype(BF16)

            @pl.loop(0, 8)
            def _(s):
                give(2 * g + i, s).start()

    @pl.when(active)
    def _():
        ring_step(1)

    ring_step(2)

    @pl.loop(3, 8)
    def _(k):
        @pl.when((k == 3) & active)
        def _():
            wait_spread((y + 3) % NY, 0)
            pass_on(0).start()
            wait_spread((y + 1) % NY, 1)
            pass_on(1).start()
            spread_x((y + 1) % NY, 1).start()
            wait_spread((y + 3) % NY, 1)
            spread_x((y + 3) % NY, 1).start()

        ring_step(k)

        @pl.when((k == 3) & jnp.logical_not(active))
        def _():
            wait_spread((y + 3) % NY, 0)
            pass_on(0).start()

        @pl.when((k == 4) & active)
        def _():
            wait_spread((y + 2) % NY, 1)
            spread_x((y + 2) % NY, 1).start()

        @pl.when(k == jnp.where(active, 4, 5))
        def _():
            experts_first()
            experts_second()

        @pl.when(k == 6)
        def _():
            for d in range(1, NY):
                src = (y + d) % NY
                remote(
                    pair_of(0), wall.at[0, src], wa_send.at[0], wa_recv.at[src], partner
                ).wait_recv()
            wall_partner.start()
            tok_across.wait_recv()
            relay.start()

        @pl.when(k == 6)
        def _():
            wait_hid((y + 3) % NY, 0)
            hid_pass(0).start()
            wait_hid((y + 1) % NY, 1)
            hid_pass(1).start()

        @pl.when(k == 7)
        def _():
            wall_partner.wait_recv()
            outputs(0)

    for p in range(2):
        go_right(7, p).wait_recv()

    local[4].wait()
    to_partner[1].wait_recv()
    relay.wait_recv()
    both = dot(tq[...], dense_w[:, 0:384])
    gu[...] = both[0:2 * NT]
    gu_send[...] = both[2 * NT:4 * NT].astype(BF16)
    gu_across = remote(gu_send, gu_recv, ac_send.at[1], ac_recv.at[1], across)
    gu_across.start()

    outputs(1)
    finish_outputs(0)

    gu_across.wait_recv()
    both = gu[...] + gu_recv[...].astype(F32)
    dense_hidden = silu(both) * pltpu.roll(both, 384 - HH, 1)
    dense_hidden = jnp.where(iota((2 * NT, 384), 1) < HH, dense_hidden, 0.0)
    hbuf[0:2 * NT] = pltpu.roll(dense_hidden, 2 * HH - 256, 1)[:, 0:256].astype(BF16)
    h_across = remote(
        hbuf.at[pl.ds(0, 2 * NT)], hbuf.at[pl.ds(2 * NT, 2 * NT)], ac_send.at[2], ac_recv.at[2],
        across,
    )
    h_across.start()

    def dense_down(t):
        for n in range(HALF // PIECE):
            cols = pl.ds(n * PIECE, PIECE)
            part = dot_nt(
                hbuf[2 * t * NT:2 * (t + 1) * NT], dense_w[n * PIECE:(n + 1) * PIECE, 256:512]
            )
            d_mine[t, :, cols] = part[0:NT]
            d_send[t, :, cols] = part[NT:2 * NT].astype(BF16)

    swaps = [
        remote(d_send.at[t], d_recv.at[t], core_send.at[6 + t], core_recv.at[6 + t], partner)
        for t in range(2)
    ]
    dense_down(0)
    swaps[0].start()

    finish_outputs(1)

    h_across.wait_recv()
    dense_down(1)
    swaps[1].start()

    def finish(t, q):
        to = 4 * xl + q
        to_x = (xl + t) % 2
        return remote(
            dterm.at[t, q], fin.at[b], fin_send.at[t * 4 + q], fin_recv.at[b],
            dev(to, to_x, z, core),
        )

    def others(t, q):
        return jnp.logical_not(own_half & (t == 0) & (4 * xl + q == b))

    for t in range(2):
        swaps[t].wait_recv()
        for n in range(2):
            cols = pl.ds(n * 2 * COLS, 2 * COLS)
            value = (d_mine[t, :, cols] + d_recv[t, :, cols].astype(F32)).astype(BF16)
            dterm[t, 2 * n] = value[:, 0:COLS]
            dterm[t, 2 * n + 1] = value[:, COLS:2 * COLS]
            for q in (2 * n, 2 * n + 1):
                @pl.when(others(t, q))
                def _():
                    finish(t, q).start()

    @pl.when(own_half)
    def _():
        fin[b] = dterm[0, b % 4]

    @pl.loop(0, EXPERTS)
    def _(e):
        remote(
            tbuf.at[0, rows_of(0, BACK)], ret.at[rows_of(e, BACK)], ret_send.at[0],
            ret_recv.at[e], partner,
        ).wait_recv()

    rows = ret[...]
    total = dot(shares[0], rows) + dot(shares[1], rows)
    total = jnp.concatenate([total[n * NT:(n + 1) * NT] for n in range(4)], axis=1)[:, 0:COLS]

    @pl.loop(0, NDP)
    def _(k):
        @pl.when(jnp.logical_not(own_half & (k == b)))
        def _():
            remote(
                dterm.at[0, 0], fin.at[k], fin_send.at[0], fin_recv.at[k], partner
            ).wait_recv()

    for k in range(NDP):
        total = total + fin[k].astype(F32)
    out[...] = total.astype(BF16)

    for copy in to_partner:
        copy.wait_send()
    for copy in (tok_across, relay, gu_across, h_across, *swaps):
        copy.wait_send()

    @pl.loop(0, 8)
    def _(n):
        dispatch(n // 4, n % 4).wait_send()

        for p in range(2):
            go_right(n, p).wait_send()

            @pl.when(n < 7)
            def _():
                go_left(n, p).wait_send()

        @pl.when(others(n // 4, n % 4))
        def _():
            finish(n // 4, n % 4).wait_send()

    @pl.loop(0, EXPERTS)
    def _(n):
        give(n // 8, n % 8).wait_send()

    wall_partner.wait_send()

    for d in range(1, NY):
        cut_to(d).wait_send()

    for g in range(2):
        cross_x(g).wait_send()
        hid_pass(g).wait_send()
        for n in range(2):
            hid_y(g, n).wait_send()

    pass_on(0).wait_send()
    for n in range(2):
        spread_y(0, n).wait_send()

    @pl.when(active)
    def _():
        spread_x(y, 0).wait_send()
        pass_on(1).wait_send()
        for n in range(2):
            spread_y(1, n).wait_send()
        for d in range(NY):
            spread_x((y + d) % NY, 1).wait_send()


def per_device(
    tokens, routes, gate_weights, w_dense_gate, w_dense_up, w_dense_down,
    w_exp_gate, w_exp_up, w_exp_down,
):
    rows = w_dense_gate.shape[0]
    vmem = pl.BlockSpec(memory_space=pltpu.VMEM)
    hbm = pl.BlockSpec(memory_space=pl.ANY)
    dma = pltpu.SemaphoreType.DMA
    return pl.pallas_call(
        kernel,
        out_shape=jax.ShapeDtypeStruct((NT, COLS), BF16),
        in_specs=[vmem] * 5 + [hbm] * 4,
        out_specs=vmem,
        scratch_shapes=[
            pltpu.VMEM((NT, D), BF16),
            pltpu.VMEM((4 * NT, HALF), BF16),
            pltpu.VMEM((2, 4 * SEND, TILE), BF16),
            pltpu.VMEM((2, 8 * SEND, TILE), BF16),
            pltpu.VMEM((TILES * BLOCK, 8 * SEND), BF16),
            pltpu.VMEM((2, 4 * NT, EXPERTS * BACK), BF16),
            pltpu.VMEM((NY * BLOCK, D), BF16),
            pltpu.VMEM((NY, 2, 2 * BLOCK, 2 * HH), BF16),
            pltpu.VMEM((2, 2 * BLOCK, COLS), F32),
            pltpu.VMEM((2, 2 * BLOCK, COLS), BF16),
            pltpu.VMEM((2, 2 * BLOCK, COLS), BF16),
            pltpu.VMEM((NY, 8 * BACK, TILE), BF16),
            pltpu.VMEM((EXPERTS * BACK, TILE), BF16),
            pltpu.VMEM((2, HH, D), BF16),
            pltpu.VMEM((2, HH, D), BF16),
            pltpu.VMEM((2, NY, HH, 2 * COLS), BF16),
            pltpu.VMEM((2, rows, CHUNK), BF16),
            pltpu.VMEM((rows, CHUNK), BF16),
            pltpu.VMEM((HALF, CHUNK), BF16),
            pltpu.VMEM((4, NY * BLOCK, HH), F32),
            pltpu.VMEM((2 * NT, 384), F32),
            pltpu.VMEM((2 * NT, 384), BF16),
            pltpu.VMEM((2 * NT, 384), BF16),
            pltpu.VMEM((4 * NT, 256), BF16),
            pltpu.VMEM((2, NT, HALF), F32),
            pltpu.VMEM((2, NT, HALF), BF16),
            pltpu.VMEM((2, NT, HALF), BF16),
            pltpu.VMEM((2, 4, NT, COLS), BF16),
            pltpu.VMEM((NDP, NT, COLS), BF16),
            dma((5,)), dma((8,)), dma((8,)), dma((3,)), dma((3,)), dma((8,)), dma((16,)),
            dma((8,)), dma((4,)), dma((2,)), dma((8,)),
            dma((16,)), dma((16,)), dma((14,)), dma((14,)),
            dma((3,)), dma((4,)), dma((2,)), dma((2,)), dma((4,)), dma((2,)), dma((8,)),
            dma((32,)), dma((32,)),
            dma((8,)), dma((8,)),
        ],
        compiler_params=pltpu.CompilerParams(
            collective_id=0, has_side_effects=True, vmem_limit_bytes=56 * 1024 * 1024
        ),
    )(
        routes.T, gate_weights.T, w_dense_gate, w_dense_up, w_dense_down.T, tokens,
        w_exp_gate[0, 0].T, w_exp_up[0, 0].T, w_exp_down[0, 0],
    )


def solution(mesh):
    in_specs = (
        P("expert", None),
        P("expert", None),
        P("expert", None),
        P("expert", "dp"),
        P("expert", "dp"),
        P("dp", "expert"),
        P("dp", "expert", None, None),
        P("dp", "expert", None, None),
        P("dp", "expert", None, None),
    )
    return jax.shard_map(
        per_device, mesh=mesh, in_specs=in_specs, out_specs=P("expert", "dp"), check_vma=False
    )
```

time: 120 us -> 110 us (0.917)
  the two profiles are of different devices: /device:TPU:43 before, /device:TPU:29 now
where the time goes in v5:
time: 110 us
  Pallas kernels  108 us (98%)
  local copies, waits for them, and re-layouts  1.67 us (2%)
    pallas_call x1, Pallas kernels, per_device(): pl.pallas_call(kernel, out_shape=jax.ShapeDtypeStruct((NT, COLS), BF16),...  108 us

profile of v5, /device:TPU:29, one launch (start us, length us, event | category | flops | bytes accessed | tf_op | source)
XLA Modules:
  0.0 109.7 jit_solution(11295852860495701800)
XLA Ops:
  0.0 108.0 %shard_map.91 = bf16[128,448]{1,0:T(8,128)(2,1)} custom-call(s32[2,128]{1,0:T(2,128)} %bitcast.14, f32[2,128]{1,0:T(2,128)} %bitcast.15, bf16[56,304]{1,0:T(8,128)(2,1)} %dg.1, bf16[56,304]{1,0:T(8,128)(2,1)} %du.1, bf16[56,304]{1,0:T(8,128)(2,1)} %bitcast.13, bf16[128,3584]{1,0:T(8,128)(2,1)} %tok_hbm.1, bf16[152,3584]{1,0:T(8,128)(2,1)} %bitcast.10, ...), custom_call_target="tpu_custom_call" | custom-call | tf_op jit(solution)/shard_map/pallas_call | solution.py:678
  108.0 1.7 %copy.10 = bf16[128,448]{0,1:T(8,128)(2,1)} copy(bf16[128,448]{1,0:T(8,128)(2,1)} %shard_map.91) | data formatting | bytes 229376 | tf_op jit(solution)/shard_map/pallas_call | solution.py:678

commit v6 on v5

--- a/solution.py
+++ b/solution.py
@@ -62,7 +62,7 @@
     acc, gu, gu_send, gu_recv, hbuf, d_mine, d_send, d_recv, dterm, fin,
     loc, core_send, core_recv, ac_send, ac_recv, dis_send, dis_recv, bx_send, by_send, bp_send, bc_recv,
     right_send, right_recv, left_send, left_recv,
-    wa_send, wa_recv, cx_send, cx_recv, hy_send, hp_send, hy_recv, ret_send, ret_recv, fin_send, fin_recv,
+    wa_send, wa_recv, cx_send, cx_recv, hy_send, hy_recv, ret_send, ret_recv, fin_send, fin_recv,
 ):
     b = lax.axis_index("dp")
     ex = lax.axis_index("expert")
@@ -277,8 +277,8 @@
 
     def spread_y(h, n):
         return remote(
-            x_part(y, h), x_part(y, h), by_send.at[2 * h + n], bc_recv.at[h * NY + y],
-            along_y(1 + 2 * n),
+            x_part(y, h), x_part(y, h), by_send.at[3 * h + n], bc_recv.at[h * NY + y],
+            along_y((1, 3, 2)[n]),
         )
 
     def pass_on(h):
@@ -339,7 +339,7 @@
                 ]
 
             spread_x(y, h).start()
-            for n in range(2):
+            for n in range(2 + h):
                 spread_y(h, n).start()
 
     relay = remote(
@@ -363,22 +363,15 @@
         wall.at[0], wall.at[1], core_send.at[4], core_recv.at[4], partner
     )
 
-    def hid_y(g, n):
+    def hid_y(g, d):
         return remote(
-            hcat.at[y, g], hcat.at[y, g], hy_send.at[2 * g + n], hy_recv.at[g * NY + y],
-            along_y(1 + 2 * n),
-        )
-
-    def hid_pass(g):
-        yy = (y + 3 - 2 * g) % NY
-        return remote(
-            hcat.at[yy, g], hcat.at[yy, g], hp_send.at[g], hy_recv.at[g * NY + yy],
-            along_y(1 + 2 * g),
+            hcat.at[y, g], hcat.at[y, g], hy_send.at[3 * g + d - 1], hy_recv.at[g * NY + y],
+            along_y(d),
         )
 
     def wait_hid(yy, g):
         remote(
-            hcat.at[yy, g], hcat.at[yy, g], hp_send.at[0], hy_recv.at[g * NY + yy], partner
+            hcat.at[yy, g], hcat.at[yy, g], hy_send.at[0], hy_recv.at[g * NY + yy], partner
         ).wait_recv()
 
     def gate_up(h):
@@ -408,8 +401,8 @@
         )
         for g in range(2):
             hcat[y, g] = hidden[g * 2 * BLOCK:(g + 1) * 2 * BLOCK]
-            for n in range(2):
-                hid_y(g, n).start()
+            for d in range(1, NY):
+                hid_y(g, d).start()
 
     wide_row = iota((8 * BACK, BLOCK), 0)
     wide_at = wide_row % BACK
@@ -430,8 +423,8 @@
         return remote(cross.at[g], crossed.at[g], cx_send.at[g], cx_recv.at[g], across_hi)
 
     def outputs(g):
-        wait_hid((y + 1 + 2 * g) % NY, g)
-        wait_hid((y + 2) % NY, g)
+        for d in range(1, NY):
+            wait_hid((y + d) % NY, g)
         total = None
         for yy in range(NY):
             value = hcat[yy, g]
@@ -475,7 +468,6 @@
             wait_spread((y + 3) % NY, 0)
             pass_on(0).start()
             wait_spread((y + 1) % NY, 1)
-            pass_on(1).start()
             spread_x((y + 1) % NY, 1).start()
             wait_spread((y + 3) % NY, 1)
             spread_x((y + 3) % NY, 1).start()
@@ -492,7 +484,7 @@
             wait_spread((y + 2) % NY, 1)
             spread_x((y + 2) % NY, 1).start()
 
-        @pl.when(k == jnp.where(active, 4, 5))
+        @pl.when(k == jnp.where(active, 5, 6))
         def _():
             experts_first()
             experts_second()
@@ -508,18 +500,6 @@
             tok_across.wait_recv()
             relay.start()
 
-        @pl.when(k == 6)
-        def _():
-            wait_hid((y + 3) % NY, 0)
-            hid_pass(0).start()
-            wait_hid((y + 1) % NY, 1)
-            hid_pass(1).start()
-
-        @pl.when(k == 7)
-        def _():
-            wall_partner.wait_recv()
-            outputs(0)
-
     for p in range(2):
         go_right(7, p).wait_recv()
 
@@ -532,8 +512,9 @@
     gu_across = remote(gu_send, gu_recv, ac_send.at[1], ac_recv.at[1], across)
     gu_across.start()
 
+    wall_partner.wait_recv()
+    outputs(0)
     outputs(1)
-    finish_outputs(0)
 
     gu_across.wait_recv()
     both = gu[...] + gu_recv[...].astype(F32)
@@ -559,15 +540,6 @@
         remote(d_send.at[t], d_recv.at[t], core_send.at[6 + t], core_recv.at[6 + t], partner)
         for t in range(2)
     ]
-    dense_down(0)
-    swaps[0].start()
-
-    finish_outputs(1)
-
-    h_across.wait_recv()
-    dense_down(1)
-    swaps[1].start()
-
     def finish(t, q):
         to = 4 * xl + q
         to_x = (xl + t) % 2
@@ -579,7 +551,7 @@
     def others(t, q):
         return jnp.logical_not(own_half & (t == 0) & (4 * xl + q == b))
 
-    for t in range(2):
+    def dense_out(t):
         swaps[t].wait_recv()
         for n in range(2):
             cols = pl.ds(n * 2 * COLS, 2 * COLS)
@@ -591,9 +563,57 @@
                 def _():
                     finish(t, q).start()
 
+    dense_down(0)
+    swaps[0].start()
+    finish_outputs(0)
+    dense_out(0)
+    finish_outputs(1)
+    h_across.wait_recv()
+    dense_down(1)
+    swaps[1].start()
+    dense_out(1)
+
     @pl.when(own_half)
     def _():
         fin[b] = dterm[0, b % 4]
+
+    for copy in to_partner:
+        copy.wait_send()
+    for copy in (tok_across, relay, gu_across, h_across, *swaps):
+        copy.wait_send()
+
+    @pl.loop(0, 8)
+    def _(n):
+        dispatch(n // 4, n % 4).wait_send()
+
+        for p in range(2):
+            go_right(n, p).wait_send()
+
+            @pl.when(n < 7)
+            def _():
+                go_left(n, p).wait_send()
+
+    wall_partner.wait_send()
+
+    for d in range(1, NY):
+        cut_to(d).wait_send()
+
+    for g in range(2):
+        cross_x(g).wait_send()
+        for d in range(1, NY):
+            hid_y(g, d).wait_send()
+
+    pass_on(0).wait_send()
+    for n in range(2):
+        spread_y(0, n).wait_send()
+
+    @pl.when(active)
+    def _():
+        spread_x(y, 0).wait_send()
+        for n in range(3):
+            spread_y(1, n).wait_send()
+        for d in range(NY):
+            spread_x((y + d) % NY, 1).wait_send()
 
     @pl.loop(0, EXPERTS)
     def _(e):
@@ -616,24 +636,10 @@
 
     for k in range(NDP):
         total = total + fin[k].astype(F32)
-    out[...] = total.astype(BF16)
-
-    for copy in to_partner:
-        copy.wait_send()
-    for copy in (tok_across, relay, gu_across, h_across, *swaps):
-        copy.wait_send()
+    out[...] = total.T.astype(BF16)
 
     @pl.loop(0, 8)
     def _(n):
-        dispatch(n // 4, n % 4).wait_send()
-
-        for p in range(2):
-            go_right(n, p).wait_send()
-
-            @pl.when(n < 7)
-            def _():
-                go_left(n, p).wait_send()
-
         @pl.when(others(n // 4, n % 4))
         def _():
             finish(n // 4, n % 4).wait_send()
@@ -641,30 +647,6 @@
     @pl.loop(0, EXPERTS)
     def _(n):
         give(n // 8, n % 8).wait_send()
-
-    wall_partner.wait_send()
-
-    for d in range(1, NY):
-        cut_to(d).wait_send()
-
-    for g in range(2):
-        cross_x(g).wait_send()
-        hid_pass(g).wait_send()
-        for n in range(2):
-            hid_y(g, n).wait_send()
-
-    pass_on(0).wait_send()
-    for n in range(2):
-        spread_y(0, n).wait_send()
-
-    @pl.when(active)
-    def _():
-        spread_x(y, 0).wait_send()
-        pass_on(1).wait_send()
-        for n in range(2):
-            spread_y(1, n).wait_send()
-        for d in range(NY):
-            spread_x((y + d) % NY, 1).wait_send()
 
 
 def per_device(
@@ -675,9 +657,9 @@
     vmem = pl.BlockSpec(memory_space=pltpu.VMEM)
     hbm = pl.BlockSpec(memory_space=pl.ANY)
     dma = pltpu.SemaphoreType.DMA
-    return pl.pallas_call(
+    out_t = pl.pallas_call(
         kernel,
-        out_shape=jax.ShapeDtypeStruct((NT, COLS), BF16),
+        out_shape=jax.ShapeDtypeStruct((COLS, NT), BF16),
         in_specs=[vmem] * 5 + [hbm] * 4,
         out_specs=vmem,
         scratch_shapes=[
@@ -711,9 +693,9 @@
             pltpu.VMEM((2, 4, NT, COLS), BF16),
             pltpu.VMEM((NDP, NT, COLS), BF16),
             dma((5,)), dma((8,)), dma((8,)), dma((3,)), dma((3,)), dma((8,)), dma((16,)),
-            dma((8,)), dma((4,)), dma((2,)), dma((8,)),
+            dma((8,)), dma((6,)), dma((2,)), dma((8,)),
             dma((16,)), dma((16,)), dma((14,)), dma((14,)),
-            dma((3,)), dma((4,)), dma((2,)), dma((2,)), dma((4,)), dma((2,)), dma((8,)),
+            dma((3,)), dma((4,)), dma((2,)), dma((2,)), dma((6,)), dma((8,)),
             dma((32,)), dma((32,)),
             dma((8,)), dma((8,)),
         ],
@@ -724,6 +706,7 @@
         routes.T, gate_weights.T, w_dense_gate, w_dense_up, w_dense_down.T, tokens,
         w_exp_gate[0, 0].T, w_exp_up[0, 0].T, w_exp_down[0, 0],
     )
+    return out_t.T
 
 
 def solution(mesh):

time: 110 us -> 110 us (level)
  the two profiles are of different devices: /device:TPU:29 before, /device:TPU:43 now
where the time goes in v6:
time: 110 us
  Pallas kernels  108 us (98%)
  local copies, waits for them, and re-layouts  1.55 us (1%)
    pallas_call x1, Pallas kernels, per_device(): pl.pallas_call(kernel, out_shape=jax.ShapeDtypeStruct((COLS, NT), BF16),...  108 us

profile of v6, /device:TPU:43, one launch (start us, length us, event | category | flops | bytes accessed | tf_op | source)
XLA Modules:
  0.0 109.7 jit_solution(7280989434840466906)
XLA Ops:
  0.0 108.1 %shard_map.91 = bf16[448,128]{1,0:T(8,128)(2,1)} custom-call(s32[2,128]{1,0:T(2,128)} %bitcast.16, f32[2,128]{1,0:T(2,128)} %bitcast.17, bf16[56,304]{1,0:T(8,128)(2,1)} %dg.1, bf16[56,304]{1,0:T(8,128)(2,1)} %du.1, bf16[56,304]{1,0:T(8,128)(2,1)} %bitcast.15, bf16[128,3584]{1,0:T(8,128)(2,1)} %tok_hbm.1, bf16[152,3584]{1,0:T(8,128)(2,1)} %bitcast.11, ...), custom_call_target="tpu_custom_call" | custom-call | tf_op jit(solution)/shard_map/pallas_call | solution.py:660
  108.1 1.6 %copy.11 = bf16[128,448]{0,1:T(8,128)(2,1)} copy(bf16[128,448]{0,1:T(8,128)(2,1)} %bitcast.14) | data formatting | bytes 229376

commit v7 on v6

--- a/solution.py
+++ b/solution.py
@@ -514,7 +514,6 @@
 
     wall_partner.wait_recv()
     outputs(0)
-    outputs(1)
 
     gu_across.wait_recv()
     both = gu[...] + gu_recv[...].astype(F32)
@@ -526,6 +525,7 @@
         across,
     )
     h_across.start()
+    outputs(1)
 
     def dense_down(t):
         for n in range(HALF // PIECE):
@@ -567,10 +567,10 @@
     swaps[0].start()
     finish_outputs(0)
     dense_out(0)
-    finish_outputs(1)
     h_across.wait_recv()
     dense_down(1)
     swaps[1].start()
+    finish_outputs(1)
     dense_out(1)
 
     @pl.when(own_half)

time: 110 us -> 107 us (0.973)
  the two profiles are of different devices: /device:TPU:43 before, /device:TPU:47 now
where the time goes in v7:
time: 107 us
  Pallas kernels  105 us (98%)
  local copies, waits for them, and re-layouts  1.55 us (1%)
    pallas_call x1, Pallas kernels, per_device(): pl.pallas_call(kernel, out_shape=jax.ShapeDtypeStruct((COLS, NT), BF16),...  105 us

profile of v7, /device:TPU:47, one launch (start us, length us, event | category | flops | bytes accessed | tf_op | source)
XLA Modules:
  0.0 106.7 jit_solution(11272797534610181953)
XLA Ops:
  0.0 105.1 %shard_map.91 = bf16[448,128]{1,0:T(8,128)(2,1)} custom-call(s32[2,128]{1,0:T(2,128)} %bitcast.16, f32[2,128]{1,0:T(2,128)} %bitcast.17, bf16[56,304]{1,0:T(8,128)(2,1)} %dg.1, bf16[56,304]{1,0:T(8,128)(2,1)} %du.1, bf16[56,304]{1,0:T(8,128)(2,1)} %bitcast.15, bf16[128,3584]{1,0:T(8,128)(2,1)} %tok_hbm.1, bf16[152,3584]{1,0:T(8,128)(2,1)} %bitcast.11, ...), custom_call_target="tpu_custom_call" | custom-call | tf_op jit(solution)/shard_map/pallas_call | solution.py:660
  105.1 1.6 %copy.11 = bf16[128,448]{0,1:T(8,128)(2,1)} copy(bf16[128,448]{0,1:T(8,128)(2,1)} %bitcast.14) | data formatting | bytes 229376
